TPU v7x, 32 devices: a whole 2x2x4 slice. The times are simulated.
32 devices in a mesh: row: 2 (over y), col: 4 (over x, core), depth: 4 (over z).
Axes of the slice: x: 2, y: 2, z: 4, core: 2. Of those that a mesh axis runs over, the one named last changes fastest.
Arguments:
- tokens: bfloat16 [2048, 5120], P(('row', 'depth'), 'col'), may hold values from -6 to 6
- w_up: bfloat16 [5120, 20480], P('col', ('row', 'depth')), may hold values from -0.078125 to 0.078125
- bias_up: float32 [20480], P(('row', 'depth')), may hold values from -3 to 3
- w_down: bfloat16 [20480, 5120], P(('row', 'depth'), 'col'), may hold values from -0.0390625 to 0.0390625
- cotangent: bfloat16 [2048, 5120], P(('row', 'depth'), 'col'), may hold values from -6 to 6
Outputs:
- input_grad: bfloat16 [2048, 5120], P(('row', 'depth'), 'col')
- up_grad: float32 [5120, 20480], P('col', ('row', 'depth'))
- up_bias_grad: float32 [20480], P(('row', 'depth'))
- down_grad: float32 [20480, 5120], P(('row', 'depth'), 'col')
- down_bias_grad: float32 [5120], P('col')
All inputs are finite; a program needn't handle non-finite values.
Results may differ from a plain program's by a relative error of at most 0.005.
Values may be sent and summed in bfloat16 or wider, within the bound.
A program may use at most 256 MiB of HBM per device.

v0:
```python
import jax
import jax.numpy as jnp
from jax import lax
from jax.sharding import PartitionSpec as P


def gelu_pair(preact):
    normal_cdf = 0.5 * (1.0 + lax.erf(preact * 0.7071067811865476))
    normal_pdf = jnp.exp(-0.5 * preact * preact) * 0.3989422804014327
    return (preact * normal_cdf, normal_cdf + preact * normal_pdf)


def times_transpose(left_rows, matrix):
    return lax.dot_general(
        left_rows, matrix, (((1,), (1,)), ((), ())), preferred_element_type=jnp.float32
    )


def over_tokens(left_rows, right_rows):
    return lax.dot_general(
        left_rows, right_rows, (((0,), (0,)), ((), ())), preferred_element_type=jnp.float32
    )


def body(tokens, w_up, bias_up, w_down, cotangent):
    token_all, cotan_all = (
        lax.all_gather(tokens, ("row", "depth"), axis=0, tiled=True),
        lax.all_gather(cotangent, ("row", "depth"), axis=0, tiled=True),
    )
    hidden_width = w_up.shape[1]
    up_rows = jnp.dot(token_all, w_up, preferred_element_type=jnp.float32)
    partials = lax.psum_scatter(
        jnp.concatenate([up_rows, times_transpose(cotan_all, w_down)], axis=1),
        "col",
        scatter_dimension=0,
        tiled=True,
    )
    activated, derivative = gelu_pair(partials[:, :hidden_width] + bias_up)
    activated_part = activated.astype(jnp.bfloat16)
    hidden_part = (partials[:, hidden_width:] * derivative).astype(jnp.bfloat16)
    activated_all, hidden_all = (
        lax.all_gather(activated_part, "col", axis=0, tiled=True),
        lax.all_gather(hidden_part, "col", axis=0, tiled=True),
    )
    down_grad = over_tokens(activated_all, cotan_all)
    up_grad = over_tokens(token_all, hidden_all)
    up_bias_grad = jnp.sum(hidden_all, axis=0, dtype=jnp.float32)
    down_bias_grad = jnp.sum(cotan_all, axis=0, dtype=jnp.float32)
    input_grad = lax.psum_scatter(
        times_transpose(hidden_all, w_up), ("row", "depth"), scatter_dimension=0, tiled=True
    )
    return (input_grad.astype(jnp.bfloat16), up_grad, up_bias_grad, down_grad, down_bias_grad)


def solution(mesh):
    return jax.shard_map(
        body,
        mesh=mesh,
        in_specs=(
            P(("row", "depth"), "col"),
            P("col", ("row", "depth")),
            P(("row", "depth")),
            P(("row", "depth"), "col"),
            P(("row", "depth"), "col"),
        ),
        out_specs=(
            P(("row", "depth"), "col"),
            P("col", ("row", "depth")),
            P(("row", "depth")),
            P(("row", "depth"), "col"),
            P("col"),
        ),
        check_vma=False,
    )
```

profile of v0, /device:TPU:0, one launch (start us, length us, event | category | flops | bytes accessed | tf_op | source)
XLA Modules:
  0.0 860.7 jit_solution(3015257230932519730)
XLA Ops:
  7.2 0.0 all-gather.7.cloned.1.call-start
  7.2 0.7 all-gather.7.cloned.1.call-update
  7.9 0.0 all-gather.5.cloned.1.call-start
  7.9 0.7 all-gather.5.cloned.1.call-update
  8.6 0.0 reduce-scatter.3.cloned.1.call-start
  8.7 90.4 %all-gather.7.cloned.1.call-done = bf16[2048,1280]{1,0:T(8,128)(2,1)} async-done(((bf16[256,1280]{1,0:T(8,128)(2,1)}), bf16[2048,1280]{1,0:T(8,128)(2,1)}) %all-gather.7.cloned.1.call-update) | async-done | bytes 5242896 | tf_op jit(solution)/shard_map/all_gather | solution.py:28
  99.1 20.4 %fusion.7 = f32[2048,2560]{1,0:T(8,128)} fusion(bf16[2048,1280]{1,0:T(8,128)(2,1)} %all-gather.7.cloned.1.call-done, bf16[2560,1280]{1,0:T(8,128)(2,1)} %param.8), kind=kOutput, calls=%fused_computation.15 | convolution fusion | flops 13421772800 | bytes 32768000 | tf_op jit(solution)/shard_map/dot_general | solution.py:14
  119.5 66.2 %all-gather.5.cloned.1.call-done = bf16[2048,1280]{1,0:T(8,128)(2,1)} async-done(((bf16[256,1280]{1,0:T(8,128)(2,1)}), bf16[2048,1280]{1,0:T(8,128)(2,1)}) %all-gather.5.cloned.1.call-update) | async-done | bytes 5242896 | tf_op jit(solution)/shard_map/all_gather | solution.py:27
  185.7 20.4 %fusion.6 = f32[2048,2560]{1,0:T(8,128)} fusion(bf16[2048,1280]{1,0:T(8,128)(2,1)} %all-gather.5.cloned.1.call-done, bf16[1280,2560]{1,0:T(8,128)(2,1)} %param.6), kind=kOutput, calls=%fused_computation.14 | convolution fusion | flops 13421772800 | bytes 32768000 | tf_op jit(solution)/shard_map/dot_general | solution.py:31
  206.1 27.7 %pad_maximum_fusion = f32[2048,5120]{1,0:T(8,128)} fusion(f32[2048,2560]{1,0:T(8,128)} %fusion.7, f32[2048,2560]{1,0:T(8,128)} %fusion.6), kind=kLoop, calls=%fused_computation | loop fusion | flops 10485760 | bytes 83886080 | tf_op jit(solution)/shard_map/concatenate | solution.py:33
  233.8 0.0 copy-start
  233.8 0.0 reduce-scatter.3.cloned.1.call-update
  233.8 0.0 all-gather.9.cloned.1.call-start
  233.8 287.0 %reduce-scatter.3.cloned.1.call-done = f32[512,5120]{1,0:T(8,128)} async-done(((f32[2048,5120]{1,0:T(8,128)}), f32[512,5120]{1,0:T(8,128)}) %reduce-scatter.3.cloned.1.call-update) | async-done | bytes 10485776 | tf_op jit(solution)/shard_map/reduce_scatter | solution.py:32
  520.8 0.0 copy-done
  520.8 6.8 multiply_convert_fusion
  527.7 0.0 all-gather.9.cloned.1.call-update
  527.7 0.0 all-gather.11.cloned.1.call-start
  527.8 0.5 all-gather.11.cloned.1.call-update
  528.3 0.2 reduce-scatter.5.cloned.1.call-start
  528.5 69.5 %all-gather.9.cloned.1.call-done = bf16[2048,2560]{1,0:T(8,128)(2,1)} async-done(((bf16[512,2560]{1,0:T(8,128)(2,1)}), bf16[2048,2560]{1,0:T(8,128)(2,1)}) %all-gather.9.cloned.1.call-update) | async-done | bytes 10485776 | tf_op jit(solution)/shard_map/all_gather | solution.py:43
  598.1 19.5 %fusion.8 = f32[2048,1280]{1,0:T(8,128)} fusion(bf16[2048,2560]{1,0:T(8,128)(2,1)} %all-gather.9.cloned.1.call-done, bf16[1280,2560]{1,0:T(8,128)(2,1)} %param.6), kind=kOutput, calls=%fused_computation.16 | convolution fusion | flops 13421772800 | bytes 27525120 | tf_op jit(solution)/shard_map/dot_general | solution.py:14
  617.5 0.0 reduce-scatter.5.cloned.1.call-update
  617.6 3.9 convert_reduce_fusion.1
  621.4 19.5 %convolution_bitcast_fusion = f32[1280,2560]{0,1:T(8,128)} fusion(bf16[2048,2560]{1,0:T(8,128)(2,1)} %all-gather.9.cloned.1.call-done, bf16[2048,1280]{1,0:T(8,128)(2,1)} %all-gather.5.cloned.1.call-done), kind=kOutput, calls=%fused_computation.2 | convolution fusion | flops 13421772800 | bytes 28835840 | tf_op jit(solution)/shard_map/dot_general | solution.py:20
  641.0 13.9 %copy.10 = f32[1280,2560]{1,0:T(8,128)} copy(f32[1280,2560]{0,1:T(8,128)} %convolution_bitcast_fusion) | data formatting | bytes 26214400
  654.9 6.1 convert_reduce_fusion
  661.0 8.8 %all-gather.11.cloned.1.call-done = bf16[2048,2560]{1,0:T(8,128)(2,1)} async-done(((bf16[512,2560]{1,0:T(8,128)(2,1)}), bf16[2048,2560]{1,0:T(8,128)(2,1)}) %all-gather.11.cloned.1.call-update) | async-done | bytes 10485776 | tf_op jit(solution)/shard_map/all_gather | solution.py:42
  669.8 19.5 %fusion.9 = f32[2560,1280]{1,0:T(8,128)} fusion(bf16[2048,2560]{1,0:T(8,128)(2,1)} %all-gather.11.cloned.1.call-done, bf16[2048,1280]{1,0:T(8,128)(2,1)} %all-gather.7.cloned.1.call-done), kind=kOutput, calls=%fused_computation.17 | convolution fusion | flops 13421772800 | bytes 28835840 | tf_op jit(solution)/shard_map/dot_general | solution.py:20
  689.3 162.3 %reduce-scatter.5.cloned.1.call-done = f32[256,1280]{1,0:T(8,128)} async-done(((f32[2048,1280]{1,0:T(8,128)}), f32[256,1280]{1,0:T(8,128)}) %reduce-scatter.5.cloned.1.call-update) | async-done | bytes 1310736 | tf_op jit(solution)/shard_map/reduce_scatter | solution.py:49
  851.6 2.2 convert_element_type.16
Async XLA Ops:
  7.2 91.9 %all-gather.7.cloned.1.call-start = ((), (), s32[]{:S(2)}) async-start(), calls=%async_computation.3 | async-start | bytes 5898240 | tf_op jit(solution)/shard_map/all_gather | solution.py:28
  7.9 177.8 %all-gather.5.cloned.1.call-start = ((), (), s32[]{:S(2)}) async-start(), calls=%async_computation.2 | async-start | bytes 5898240 | tf_op jit(solution)/shard_map/all_gather | solution.py:27
  8.6 512.2 %reduce-scatter.3.cloned.1.call-start = ((), (), s32[]{:S(2)}) async-start(), calls=%async_computation.4 | async-start | bytes 52428800 | tf_op jit(solution)/shard_map/reduce_scatter | solution.py:32
  233.8 287.1 %copy-start = (f32[2560]{0:T(1024)S(1)}, f32[2560]{0:T(1024)}, u32[]{:S(2)}) copy-start(f32[2560]{0:T(1024)} %param.7) | copy-start | bytes 30724
  233.8 364.3 %all-gather.9.cloned.1.call-start = ((), (), s32[]{:S(2)}) async-start(), calls=%async_computation.5 | async-start | bytes 13107200 | tf_op jit(solution)/shard_map/all_gather | solution.py:43
  527.7 142.1 %all-gather.11.cloned.1.call-start = ((), (), s32[]{:S(2)}) async-start(), calls=%async_computation.7 | async-start | bytes 13107200 | tf_op jit(solution)/shard_map/all_gather | solution.py:42
  528.3 323.3 %reduce-scatter.5.cloned.1.call-start = ((), (), s32[]{:S(2)}) async-start(), calls=%async_computation.6 | async-start | bytes 11796480 | tf_op jit(solution)/shard_map/reduce_scatter | solution.py:49
Sparse Core Ops, SparseCore 0:
  10.1 88.9 all-gather.6
  101.2 84.4 all-gather.4
  233.9 286.8 reduce-scatter.2
  527.8 70.2 all-gather.8
  599.6 70.1 all-gather.10
  673.6 177.9 reduce-scatter.4
where the time goes:
time: 861 us
  waiting for transfers between devices  686 us (80%)
  matrix products  99.4 us (12%)
  other arithmetic  46.7 us (5%)
  between operations  14.1 us (2%)
  local copies, waits for them, and re-layouts  13.9 us (2%)
    reduce_scatter x1, waiting for transfers between devices, body(): lax.psum_scatter(jnp.concatenate([up_rows, times_transpose(cotan_all, w_d...  287 us
    reduce_scatter x1, waiting for transfers between devices, body(): lax.psum_scatter(times_transpose(hidden_all, w_up), ('row', 'depth'), sca...  162 us
    all_gather x1, waiting for transfers between devices, body(): lax.all_gather(cotangent, ('row', 'depth'), axis=0, tiled=True)  90.4 us
    all_gather x1, waiting for transfers between devices, body(): lax.all_gather(hidden_part, 'col', axis=0, tiled=True)  69.5 us
    all_gather x1, waiting for transfers between devices, body(): lax.all_gather(tokens, ('row', 'depth'), axis=0, tiled=True)  66.2 us
    dot_general x2, matrix products, times_transpose(): lax.dot_general(left_rows, matrix, (((1,), (1,)), ((), ())), preferred_el...  39.9 us
    dot_general x2, matrix products, over_tokens(): lax.dot_general(left_rows, right_rows, (((0,), (0,)), ((), ())), preferre...  39.1 us
    concatenate x1, other arithmetic, body(): jnp.concatenate([up_rows, times_transpose(cotan_all, w_down)], axis=1)  27.7 us
  transfers between devices with their start and end apart: 6, of which 6 were waited for; matrix products, arithmetic and copies ran while one was open for 12% of the time, Pallas kernels for 0%

commit v1 on v0

v1 whole, which is shorter than its diff:
```python
import jax
import jax.numpy as jnp
from jax import lax
from jax.sharding import PartitionSpec as P

CHUNKS = ("own", 0, 1, 2, 3)
PIECES = 4
GROUPS = ((0, 1, 2), (3, 4))


def gelu_pair(preact):
    normal_cdf = 0.5 * (1.0 + lax.erf(preact * 0.7071067811865476))
    normal_pdf = jnp.exp(-0.5 * preact * preact) * 0.3989422804014327
    return (preact * normal_cdf, normal_cdf + preact * normal_pdf)


def times_transpose(left_rows, matrix):
    return lax.dot_general(
        left_rows, matrix, (((1,), (1,)), ((), ())), preferred_element_type=jnp.float32
    )


def over_tokens(left_rows, right_rows):
    return lax.dot_general(
        left_rows, right_rows, (((0,), (0,)), ((), ())), preferred_element_type=jnp.float32
    )


def swap(array, bit, axis="col"):
    pairs = [(i, i ^ bit) for i in range(lax.axis_size(axis))]
    return lax.ppermute(array, axis, pairs)


def steps():
    return [
        (1 << k, axis) for axis in ("depth", "row") for k in range(lax.axis_size(axis).bit_length() - 1)
    ]


def quarter(array, index):
    rows = array.shape[0] // 4
    return lax.dynamic_slice_in_dim(array, index * rows, rows, 0)


def after(array, *earlier):
    return lax.optimization_barrier((array, earlier))[0]


def over_cores(partial):
    half = partial.shape[0] // 2
    return partial[:half] + swap(partial[half:].astype(jnp.bfloat16), 1).astype(jnp.float32)


def over_chips(partial):
    half = partial.shape[0] // 2
    return partial[:half] + swap(partial[half:].astype(jnp.bfloat16), 2).astype(jnp.float32)


def spread(mine):
    both = jnp.concatenate([mine, swap(mine, 2)], axis=0)
    return jnp.concatenate([both, swap(both, 1)], axis=0)


def gather_others(block):
    exchanges = steps()
    for bit, axis in exchanges[:-1]:
        block = jnp.concatenate([block, swap(block, bit, axis)], axis=2)
    return jnp.concatenate([block[:, :, 1:], swap(block, *exchanges[-1])], axis=2), block


def scatter_others(part):
    total = None
    for bit, axis in reversed(steps()):
        if total is None:
            half = (part.shape[1] + 1) // 2
            got = swap(part[:, half - 1 :].astype(jnp.bfloat16), bit, axis).astype(jnp.float32)
            total = jnp.concatenate([got[:, :1], got[:, 1:] + part[:, : half - 1]], axis=1)
        else:
            half = total.shape[1] // 2
            kind = jnp.bfloat16 if half > 1 else jnp.float32
            total = total[:, :half] + swap(total[:, half:].astype(kind), bit, axis).astype(jnp.float32)
    return total


def body(tokens, w_up, bias_up, w_down, cotangent):
    me = lax.axis_index("col")
    rows, width = tokens.shape
    order = (0, 2, 1, 3)
    fourth = rows // 4

    def relative(array):
        return jnp.stack([quarter(array, me ^ j) for j in order])

    local = jnp.stack([relative(tokens), relative(cotangent)])
    last = len(CHUNKS) - 1
    stacked, blocks, gathered = [], [], None
    for chunk in CHUNKS:
        if chunk == "own":
            stacked.append(local)
        else:
            piece = slice(fourth * chunk // PIECES, fourth * (chunk + 1) // PIECES)
            block = local[:, :, None, piece]
            if gathered is not None:
                block = after(block, gathered)
            whole, gathered = gather_others(block)
            stacked.append(whole)

    token_parts, cotan_parts, sums, pairs, hidden_parts, activated_parts, grads = [], [], [], [], [], [], []
    input_own, input_others = None, []

    def forward(i):
        both = stacked[i].reshape(2, -1, width)
        if i >= 1:
            both = after(both, *sums[i - 1])
        if i >= 2:
            both = after(both, *pairs[i - 2])
        if i >= 3:
            both = after(both, hidden_parts[i - 3], activated_parts[i - 3])
        token_rows, cotan_rows = both
        token_parts.append(token_rows)
        cotan_parts.append(cotan_rows)
        preact = over_cores(jnp.dot(token_rows, w_up, preferred_element_type=jnp.float32))
        back = over_cores(times_transpose(cotan_rows, w_down))
        sums.append((preact, back))

    def middle(i):
        preact, back = (over_chips(partial) for partial in sums[i])
        if i == last:
            preact = after(preact, *grads[0])
        activated, derivative = gelu_pair(preact + bias_up)
        pairs.append((activated.astype(jnp.bfloat16), (back * derivative).astype(jnp.bfloat16)))

    def backward(i):
        nonlocal input_own
        activated, hidden = pairs[i]
        hidden_parts.append(spread(hidden))
        activated_parts.append(spread(activated))
        part = times_transpose(hidden_parts[i], w_up)
        if CHUNKS[i] == "own":
            input_own = part.reshape(4, fourth, width)
        else:
            part = part.reshape(stacked[i].shape[1:])
            input_others.append(scatter_others(part).reshape(4, -1, width))
        for group in GROUPS:
            if i == group[-1]:
                token_rows, cotan_rows, hidden_rows, activated_rows = (
                    jnp.concatenate([parts[i] for i in group], axis=0)
                    for parts in (token_parts, cotan_parts, hidden_parts, activated_parts)
                )
                grads.append(
                    (
                        over_tokens(token_rows, hidden_rows),
                        jnp.sum(hidden_rows, axis=0, dtype=jnp.float32),
                        over_tokens(activated_rows, cotan_rows),
                        jnp.sum(cotan_rows, axis=0, dtype=jnp.float32),
                    )
                )

    for i in range(last + 3):
        if i <= last:
            forward(i)
        if 1 <= i <= last + 1:
            middle(i - 1)
        if i >= 2:
            backward(i - 2)
    up_grad, up_bias_grad, down_grad, down_bias_grad = (sum(parts) for parts in zip(*grads))
    input_grad = (input_own + jnp.concatenate(input_others, axis=1)).astype(jnp.bfloat16)
    input_grad = input_grad.reshape(rows, width)
    input_grad = jnp.concatenate(
        [quarter(input_grad, (2 * (j & 1)) | (j >> 1)) for j in [me ^ q for q in range(4)]], axis=0
    )
    return (input_grad, up_grad, up_bias_grad, down_grad, down_bias_grad)


def solution(mesh):
    return jax.shard_map(
        body,
        mesh=mesh,
        in_specs=(
            P(("row", "depth"), "col"),
            P("col", ("row", "depth")),
            P(("row", "depth")),
            P(("row", "depth"), "col"),
            P(("row", "depth"), "col"),
        ),
        out_specs=(
            P(("row", "depth"), "col"),
            P("col", ("row", "depth")),
            P(("row", "depth")),
            P(("row", "depth"), "col"),
            P("col"),
        ),
        check_vma=False,
    )
```

time: 861 us -> 516 us (0.60)
  waiting for transfers between devices: 686 us -> 241 us
  starting transfers between devices: 0.42 us -> 54.9 us
  matrix products: 99.4 us -> 130 us
  local copies, waits for them, and re-layouts: 13.9 us -> 43.4 us
  between operations: 14.1 us -> 2.06 us
    reduce_scatter x2 -> x0, waiting for transfers between devices: 449 us -> none  [the longest x1 287 us: body(): lax.psum_scatter(jnp.concatenate([up_rows, times_transpose(cotan_all, w_d...]
    ppermute x0 -> x64, waiting for transfers between devices: none -> 241 us  [swap(): return lax.ppermute(array, axis, pairs)]
    all_gather x4 -> x0, waiting for transfers between devices: 235 us -> none  [the longest x1 90.4 us: body(): lax.all_gather(cotangent, ('row', 'depth'), axis=0, tiled=True)]
    ppermute x0 -> x64, starting transfers between devices: none -> 54.9 us  [swap(): return lax.ppermute(array, axis, pairs)]
    dot_general x2 -> x4, matrix products: 39.1 us -> 53 us  [over_tokens(): lax.dot_general(left_rows, right_rows, (((0,), (0,)), ((), ())), preferre...]
    dot_general x2 -> x10, matrix products: 39.9 us -> 51.8 us  [times_transpose(): lax.dot_general(left_rows, matrix, (((1,), (1,)), ((), ())), preferred_el...]
    concatenate x1 -> x22, other arithmetic: 27.7 us -> 16.1 us  [the longest x10 6.89 us: spread(): both = jnp.concatenate([mine, swap(mine, 2)], axis=0)]
    slice x0 -> x36, local copies, waits for them, and re-layouts: none -> 11.1 us  [the longest x10 6.06 us: over_chips(): partial[half:].astype(jnp.bfloat16)]
  transfers between devices with their start and end apart: 6 -> 64, of which waited for: 6 -> 27; matrix products, arithmetic and copies ran while one was open for 12% -> 39% of each run, Pallas kernels for 0% -> 0%
where the time goes in v1:
time: 516 us; the launch traced here: 510 us
  waiting for transfers between devices  241 us (47%)
  matrix products  130 us (25%)
  starting transfers between devices  54.9 us (11%)
  local copies, waits for them, and re-layouts  43.4 us (8%)
  other arithmetic  39.7 us (8%)
    ppermute x64, waiting for transfers between devices, swap(): return lax.ppermute(array, axis, pairs)  241 us
    ppermute x64, starting transfers between devices, swap(): return lax.ppermute(array, axis, pairs)  54.9 us
    dot_general x4, matrix products, over_tokens(): lax.dot_general(left_rows, right_rows, (((0,), (0,)), ((), ())), preferre...  53 us
    dot_general x10, matrix products, times_transpose(): lax.dot_general(left_rows, matrix, (((1,), (1,)), ((), ())), preferred_el...  51.8 us
    dot_general x5, matrix products, forward(): jnp.dot(token_rows, w_up, preferred_element_type=jnp.float32)  25 us
    unnamed x84, local copies, waits for them, and re-layouts  19 us
  transfers between devices with their start and end apart: 64, of which 27 were waited for; matrix products, arithmetic and copies ran while one was open for 39% of the time, Pallas kernels for 0%

profile of v1, /device:TPU:0, one launch (start us, length us, event | category | flops | bytes accessed | tf_op | source)
XLA Modules:
  0.0 510.4 jit_solution(2995241397507890021)
XLA Ops:
  3.4 3.0 collective-permute-start.6
  11.0 3.1 collective-permute-done.6
  15.0 2.8 collective-permute-start.7
  21.6 24.5 %collective-permute-done.7 = bf16[2,4,2,16,1280]{4,3,2,1,0:T(8,128)(2,1)} collective-permute-done((bf16[2,4,2,16,1280]{4,3,2,1,0:T(8,128)(2,1)}, bf16[2,4,2,16,1280]{4,3,2,1,0:T(8,128)(2,1)}, u32[]{:S(2)}, u32[]{:S(2)}) %collective-permute-start.7) | collective-permute-done | bytes 655392 | tf_op jit(solution)/shard_map/ppermute | solution.py:31
  56.3 3.2 collective-permute-start.19
  61.1 5.6 %collective-permute-done.49 = bf16[64,2560]{1,0:T(8,128)(2,1)S(1)} collective-permute-done((bf16[64,2560]{1,0:T(8,128)(2,1)S(1)}, bf16[64,2560]{1,0:T(8,128)(2,1)S(1)}, u32[]{:S(2)}, u32[]{:S(2)}) %collective-permute-start.49) | collective-permute-done | bytes 327712 | tf_op jit(solution)/shard_map/ppermute | solution.py:31
  68.4 19.6 %collective-permute-done.19 = bf16[2,4,2,16,1280]{4,3,1,0,2:T(8,128)(2,1)S(1)} collective-permute-done((bf16[2,4,2,16,1280]{4,3,1,0,2:T(8,128)(2,1)S(1)}, bf16[2,4,2,16,1280]{4,3,1,0,2:T(8,128)(2,1)S(1)}, u32[]{:S(2)}, u32[]{:S(2)}) %collective-permute-start.19) | collective-permute-done | bytes 655392 | tf_op jit(solution)/shard_map/ppermute | solution.py:31
  92.8 6.0 %collective-permute-done.30 = bf16[2,4,1,16,1280]{4,3,1,0,2:T(8,128)(2,1)S(1)} collective-permute-done((bf16[2,4,1,16,1280]{4,3,1,0,2:T(8,128)(2,1)S(1)}, bf16[2,4,1,16,1280]{4,3,1,0,2:T(8,128)(2,1)S(1)}, u32[]{:S(2)}, u32[]{:S(2)}) %collective-permute-start.30) | collective-permute-done | bytes 327712 | tf_op jit(solution)/shard_map/ppermute | solution.py:31
  98.9 3.2 collective-permute-start.31
  103.4 5.5 %fusion.85 = f32[448,2560]{1,0:T(8,128)S(1)} fusion(bf16[2560,1280]{1,0:T(8,128)(2,1)} %param.8, bf16[2,448,1280]{2,1,0:T(8,128)(2,1)S(1)} %bitcast.101), kind=kOutput, calls=%fused_computation.258 | convolution fusion | flops 2936012800 | bytes 12288000 | tf_op jit(solution)/shard_map/dot_general | solution.py:18
  108.9 5.3 %fusion.86 = f32[448,2560]{1,0:T(8,128)S(1)} fusion(bf16[1280,2560]{1,0:T(8,128)(2,1)} %param.6, bf16[2,448,1280]{2,1,0:T(8,128)(2,1)S(1)} %bitcast.102), kind=kOutput, calls=%fused_computation.259 | convolution fusion | flops 2936012800 | bytes 12288000 | tf_op jit(solution)/shard_map/dot_general | solution.py:122
  115.2 15.0 %collective-permute-done.31 = bf16[2,4,2,16,1280]{4,3,1,0,2:T(8,128)(2,1)S(1)} collective-permute-done((bf16[2,4,2,16,1280]{4,3,1,0,2:T(8,128)(2,1)S(1)}, bf16[2,4,2,16,1280]{4,3,1,0,2:T(8,128)(2,1)S(1)}, u32[]{:S(2)}, u32[]{:S(2)}) %collective-permute-start.31) | collective-permute-done | bytes 655392 | tf_op jit(solution)/shard_map/ppermute | solution.py:31
  134.0 5.7 %collective-permute-done.42 = bf16[2,4,1,16,1280]{4,3,1,0,2:T(8,128)(2,1)S(1)} collective-permute-done((bf16[2,4,1,16,1280]{4,3,1,0,2:T(8,128)(2,1)S(1)}, bf16[2,4,1,16,1280]{4,3,1,0,2:T(8,128)(2,1)S(1)}, u32[]{:S(2)}, u32[]{:S(2)}) %collective-permute-start.42) | collective-permute-done | bytes 327712 | tf_op jit(solution)/shard_map/ppermute | solution.py:31
  139.8 3.3 collective-permute-start.43
  144.6 5.3 %fusion.87 = f32[448,2560]{1,0:T(8,128)S(1)} fusion(bf16[2560,1280]{1,0:T(8,128)(2,1)} %param.8, bf16[2,448,1280]{2,1,0:T(8,128)(2,1)S(1)} %bitcast.98), kind=kOutput, calls=%fused_computation.260 | convolution fusion | flops 2936012800 | bytes 12288000 | tf_op jit(solution)/shard_map/dot_general | solution.py:18
  149.9 5.3 %fusion.88 = f32[448,2560]{1,0:T(8,128)S(1)} fusion(bf16[1280,2560]{1,0:T(8,128)(2,1)} %param.6, bf16[2,448,1280]{2,1,0:T(8,128)(2,1)S(1)} %bitcast.99), kind=kOutput, calls=%fused_computation.261 | convolution fusion | flops 2936012800 | bytes 12288000 | tf_op jit(solution)/shard_map/dot_general | solution.py:122
  159.3 11.9 %collective-permute-done.10 = bf16[112,2560]{1,0:T(8,128)(2,1)S(1)} collective-permute-done((bf16[112,2560]{1,0:T(8,128)(2,1)S(1)}, bf16[112,2560]{1,0:T(8,128)(2,1)S(1)}, u32[]{:S(2)}, u32[]{:S(2)}) %collective-permute-start.10) | collective-permute-done | bytes 573472 | tf_op jit(solution)/shard_map/ppermute | solution.py:31
  171.2 10.5 %collective-permute-done.12 = bf16[112,2560]{1,0:T(8,128)(2,1)S(1)} collective-permute-done((bf16[112,2560]{1,0:T(8,128)(2,1)}, bf16[112,2560]{1,0:T(8,128)(2,1)S(1)}, u32[]{:S(2)}, u32[]{:S(2)}) %collective-permute-start.12) | collective-permute-done | bytes 573472 | tf_op jit(solution)/shard_map/ppermute | solution.py:31
  188.9 10.5 %collective-permute-done.13 = bf16[112,2560]{1,0:T(8,128)(2,1)S(1)} collective-permute-done((bf16[112,2560]{1,0:T(8,128)(2,1)S(1)}, bf16[112,2560]{1,0:T(8,128)(2,1)S(1)}, u32[]{:S(2)}, u32[]{:S(2)}) %collective-permute-start.13) | collective-permute-done | bytes 573472 | tf_op jit(solution)/shard_map/ppermute | solution.py:31
  202.9 5.3 %fusion.89 = f32[448,2560]{1,0:T(8,128)S(1)} fusion(bf16[2560,1280]{1,0:T(8,128)(2,1)} %param.8, bf16[2,448,1280]{2,1,0:T(8,128)(2,1)S(1)} %bitcast.95), kind=kOutput, calls=%fused_computation.262 | convolution fusion | flops 2936012800 | bytes 12288000 | tf_op jit(solution)/shard_map/dot_general | solution.py:18
  208.3 6.9 %fusion.90 = f32[448,2560]{1,0:T(8,128)S(1)} fusion(bf16[1280,2560]{1,0:T(8,128)(2,1)} %param.6, bf16[2,448,1280]{2,1,0:T(8,128)(2,1)S(1)} %bitcast.96), kind=kOutput, calls=%fused_computation.263 | convolution fusion | flops 2936012800 | bytes 12288000 | tf_op jit(solution)/shard_map/dot_general | solution.py:122
  226.4 7.6 %fusion.95 = f32[448,1280]{1,0:T(8,128)} fusion(bf16[1280,2560]{1,0:T(8,128)(2,1)} %param.6, bf16[224,2560]{1,0:T(8,128)(2,1)S(1)} %collective-permute-done.14, bf16[112,2560]{1,0:T(8,128)(2,1)S(1)} %copy-done.7, bf16[112,2560]{1,0:T(8,128)(2,1)S(1)} %get-tuple-element.48), kind=kOutput, calls=%fused_computation.268 | convolution fusion | flops 2942894080 | bytes 11141120 | tf_op jit(solution)/shard_map/dot_general | solution.py:18
  246.3 12.2 %collective-permute-done.34 = bf16[112,2560]{1,0:T(8,128)(2,1)S(1)} collective-permute-done((bf16[112,2560]{1,0:T(8,128)(2,1)S(1)}, bf16[112,2560]{1,0:T(8,128)(2,1)S(1)}, u32[]{:S(2)}, u32[]{:S(2)}) %collective-permute-start.34) | collective-permute-done | bytes 573472 | tf_op jit(solution)/shard_map/ppermute | solution.py:31
  258.5 11.3 %collective-permute-done.36 = bf16[112,2560]{1,0:T(8,128)(2,1)S(1)} collective-permute-done((bf16[112,2560]{1,0:T(8,128)(2,1)S(1)}, bf16[112,2560]{1,0:T(8,128)(2,1)S(1)}, u32[]{:S(2)}, u32[]{:S(2)}) %collective-permute-start.36) | collective-permute-done | bytes 573472 | tf_op jit(solution)/shard_map/ppermute | solution.py:31
  269.8 3.4 constant_dynamic-update-slice_fusion.35
  275.2 5.3 %fusion.91 = f32[448,2560]{1,0:T(8,128)S(1)} fusion(bf16[2560,1280]{1,0:T(8,128)(2,1)} %param.8, bf16[2,448,1280]{2,1,0:T(8,128)(2,1)S(1)} %bitcast.92), kind=kOutput, calls=%fused_computation.264 | convolution fusion | flops 2936012800 | bytes 12288000 | tf_op jit(solution)/shard_map/dot_general | solution.py:18
  280.6 5.7 %fusion.92 = f32[448,2560]{1,0:T(8,128)S(1)} fusion(bf16[1280,2560]{1,0:T(8,128)(2,1)} %param.6, bf16[2,448,1280]{2,1,0:T(8,128)(2,1)S(1)} %bitcast.93), kind=kOutput, calls=%fused_computation.265 | convolution fusion | flops 2936012800 | bytes 12288000 | tf_op jit(solution)/shard_map/dot_general | solution.py:122
  292.8 11.3 %collective-permute-done.16 = bf16[4,2,16,1280]{3,2,0,1:T(8,128)(2,1)S(1)} collective-permute-done((bf16[4,2,16,1280]{3,2,0,1:T(8,128)(2,1)S(1)}, bf16[4,2,16,1280]{3,2,0,1:T(8,128)(2,1)S(1)}, u32[]{:S(2)}, u32[]{:S(2)}) %collective-permute-start.16) | collective-permute-done | bytes 327712 | tf_op jit(solution)/shard_map/ppermute | solution.py:31
  304.2 9.5 %collective-permute-done.60 = bf16[112,2560]{1,0:T(8,128)(2,1)S(1)} collective-permute-done((bf16[112,2560]{1,0:T(8,128)(2,1)S(1)}, bf16[112,2560]{1,0:T(8,128)(2,1)S(1)}, u32[]{:S(2)}, u32[]{:S(2)}) %collective-permute-start.60) | collective-permute-done | bytes 573472 | tf_op jit(solution)/shard_map/ppermute | solution.py:31
  314.8 9.3 %collective-permute-done.37 = bf16[112,2560]{1,0:T(8,128)(2,1)S(1)} collective-permute-done((bf16[112,2560]{1,0:T(8,128)(2,1)S(1)}, bf16[112,2560]{1,0:T(8,128)(2,1)S(1)}, u32[]{:S(2)}, u32[]{:S(2)}) %collective-permute-start.37) | collective-permute-done | bytes 573472 | tf_op jit(solution)/shard_map/ppermute | solution.py:31
  336.9 6.4 %fusion.13 = f32[448,1280]{1,0:T(8,128)S(1)} fusion(bf16[1280,2560]{1,0:T(8,128)(2,1)} %param.6, bf16[224,2560]{1,0:T(8,128)(2,1)} %collective-permute-done.38, bf16[112,2560]{1,0:T(8,128)(2,1)S(1)} %collective-permute-done.37, bf16[112,2560]{1,0:T(8,128)(2,1)S(1)} %get-tuple-element.52), kind=kOutput, calls=%fused_computation.41 | convolution fusion | flops 2942894080 | bytes 11141120 | tf_op jit(solution)/shard_map/dot_general | solution.py:18
  347.7 12.9 %fusion = f32[1280,2560]{1,0:T(8,128)} fusion(bf16[1152,2560]{1,0:T(8,128)(2,1)S(1)} %constant_dynamic-update-slice_fusion.6, bf16[448,1280]{1,0:T(8,128)(2,1)S(1)} %copy-done.16, bf16[448,1280]{1,0:T(8,128)(2,1)S(1)} %copy-done.15, bf16[256,1280]{1,0:T(8,128)(2,1)} %bitcast.119), kind=kOutput, calls=%fused_computation.6 | convolution fusion | flops 7558594560 | bytes 21954560 | tf_op jit(solution)/shard_map/dot_general | solution.py:24
  360.6 2.3 constant_dynamic-update-slice_fusion.15
  363.0 13.8 %fusion.28 = f32[2560,1280]{1,0:T(8,128)} fusion(bf16[1152,2560]{1,0:T(8,128)(2,1)} %constant_dynamic-update-slice_fusion.15, bf16[448,1280]{1,0:T(8,128)(2,1)S(1)} %get-tuple-element.63, bf16[448,1280]{1,0:T(8,128)(2,1)S(1)} %get-tuple-element.61, bf16[256,1280]{1,0:T(8,128)(2,1)S(1)} %bitcast.106), kind=kOutput, calls=%fused_computation.80 | convolution fusion | flops 7558594560 | bytes 21954560 | tf_op jit(solution)/shard_map/dot_general | solution.py:24
  379.3 2.4 constant_dynamic-update-slice_fusion.33
  381.7 2.5 constant_dynamic-update-slice_fusion.32
  386.2 6.4 %fusion.7 = f32[448,1280]{1,0:T(8,128)S(1)} fusion(bf16[1280,2560]{1,0:T(8,128)(2,1)} %param.6, bf16[224,2560]{1,0:T(8,128)(2,1)} %collective-permute-done.26, bf16[112,2560]{1,0:T(8,128)(2,1)S(1)} %collective-permute-done.25, bf16[112,2560]{1,0:T(8,128)(2,1)S(1)} %get-tuple-element.92), kind=kOutput, calls=%fused_computation.34 | convolution fusion | flops 2942894080 | bytes 11141120 | tf_op jit(solution)/shard_map/dot_general | solution.py:18
  394.3 16.2 %collective-permute-done.55 = bf16[112,2560]{1,0:T(8,128)(2,1)S(1)} collective-permute-done((bf16[112,2560]{1,0:T(8,128)(2,1)S(1)}, bf16[112,2560]{1,0:T(8,128)(2,1)S(1)}, u32[]{:S(2)}, u32[]{:S(2)}) %collective-permute-start.55) | collective-permute-done | bytes 573472 | tf_op jit(solution)/shard_map/ppermute | solution.py:31
  413.2 2.7 collective-permute-start.28
  416.0 22.1 %collective-permute-done.40 = bf16[4,2,16,1280]{3,2,0,1:T(8,128)(2,1)S(1)} collective-permute-done((bf16[4,2,16,1280]{3,2,0,1:T(8,128)(2,1)S(1)}, bf16[4,2,16,1280]{3,2,0,1:T(8,128)(2,1)S(1)}, u32[]{:S(2)}, u32[]{:S(2)}) %collective-permute-start.40) | collective-permute-done | bytes 327712 | tf_op jit(solution)/shard_map/ppermute | solution.py:31
  438.3 6.0 %collective-permute-done.28 = bf16[4,2,16,1280]{3,2,0,1:T(8,128)(2,1)S(1)} collective-permute-done((bf16[4,2,16,1280]{3,2,0,1:T(8,128)(2,1)S(1)}, bf16[4,2,16,1280]{3,2,0,1:T(8,128)(2,1)S(1)}, u32[]{:S(2)}, u32[]{:S(2)}) %collective-permute-start.28) | collective-permute-done | bytes 327712 | tf_op jit(solution)/shard_map/ppermute | solution.py:31
  444.5 6.8 %collective-permute-done.41 = f32[4,1,16,1280]{3,2,0,1:T(8,128)S(1)} collective-permute-done((f32[4,1,16,1280]{3,2,0,1:T(8,128)S(1)}, f32[4,1,16,1280]{3,2,0,1:T(8,128)S(1)}, u32[]{:S(2)}, u32[]{:S(2)}) %collective-permute-start.41) | collective-permute-done | bytes 327712 | tf_op jit(solution)/shard_map/ppermute | solution.py:31
  451.4 6.9 %collective-permute-done.29 = f32[4,1,16,1280]{3,2,0,1:T(8,128)S(1)} collective-permute-done((f32[4,1,16,1280]{3,2,0,1:T(8,128)S(1)}, f32[4,1,16,1280]{3,2,0,1:T(8,128)S(1)}, u32[]{:S(2)}, u32[]{:S(2)}) %collective-permute-start.29) | collective-permute-done | bytes 327712 | tf_op jit(solution)/shard_map/ppermute | solution.py:31
  458.3 3.1 fusion.19
  463.3 13.3 %convolution_add_fusion.1 = f32[1280,2560]{1,0:T(8,128)} fusion(f32[1280,2560]{1,0:T(8,128)} %fusion, bf16[896,2560]{1,0:T(8,128)(2,1)S(1)} %constant_dynamic-update-slice_fusion.24, bf16[448,1280]{1,0:T(8,128)(2,1)S(1)} %copy-done.17, bf16[448,1280]{1,0:T(8,128)(2,1)S(1)} %copy-done.14), kind=kOutput, calls=%fused_computation.1 | convolution fusion | flops 5879889920 | bytes 33095680 | tf_op jit(solution)/shard_map/dot_general | solution.py:24
  480.7 13.0 %convolution_add_fusion = f32[2560,1280]{1,0:T(8,128)} fusion(f32[2560,1280]{1,0:T(8,128)} %fusion.28, bf16[896,2560]{1,0:T(8,128)(2,1)S(1)} %copy-done.22, bf16[448,1280]{1,0:T(8,128)(2,1)S(1)} %get-tuple-element.59, bf16[448,1280]{1,0:T(8,128)(2,1)S(1)} %get-tuple-element.57), kind=kOutput, calls=%fused_computation | convolution fusion | flops 5879889920 | bytes 33095680 | tf_op jit(solution)/shard_map/dot_general | solution.py:24
  495.9 8.3 %collective-permute-done.59 = f32[4,1,16,1280]{3,2,0,1:T(8,128)S(1)} collective-permute-done((f32[4,1,16,1280]{3,2,0,1:T(8,128)S(1)}, f32[4,1,16,1280]{3,2,0,1:T(8,128)S(1)}, u32[]{:S(2)}, u32[]{:S(2)}) %collective-permute-start.59) | collective-permute-done | bytes 327712 | tf_op jit(solution)/shard_map/ppermute | solution.py:31
  504.4 4.8 fusion.6
  (299 shorter events, 121.1 us)
Async XLA Ops:
  15.0 31.2 %collective-permute-start.7 = (bf16[2,4,2,16,1280]{4,3,2,1,0:T(8,128)(2,1)}, bf16[2,4,2,16,1280]{4,3,2,1,0:T(8,128)(2,1)}, u32[]{:S(2)}, u32[]{:S(2)}) collective-permute-start(bf16[2,4,2,16,1280]{4,3,2,1,0:T(8,128)(2,1)} %pad_maximum_fusion.28), channel_id=1, source_target_pairs={{0,2},{1,3},{2,0},{3,1},{4,6},{5,7},{6,4},{7,5},{8,10},{9,11},{10,... | collective-permute-start | bytes 1966088 | tf_op jit(solution)/shard_map/ppermute | solution.py:31
  18.7 29.4 %collective-permute-start.1 = (bf16[64,2560]{1,0:T(8,128)(2,1)}, bf16[64,2560]{1,0:T(8,128)(2,1)}, u32[]{:S(2)}, u32[]{:S(2)}) collective-permute-start(bf16[64,2560]{1,0:T(8,128)(2,1)} %slice.581), channel_id=1, source_target_pairs={{0,8},{4,12},{8,0},{12,4},{1,9},{5,13},{9,1},{13,5},{2,10},{6,14},... | collective-permute-start | bytes 983048 | tf_op jit(solution)/shard_map/ppermute | solution.py:31
  21.1 27.0 %collective-permute-start.3 = (bf16[64,2560]{1,0:T(8,128)(2,1)}, bf16[64,2560]{1,0:T(8,128)(2,1)}, u32[]{:S(2)}, u32[]{:S(2)}) collective-permute-start(bf16[64,2560]{1,0:T(8,128)(2,1)} %slice.580), channel_id=1, source_target_pairs={{0,8},{4,12},{8,0},{12,4},{1,9},{5,13},{9,1},{13,5},{2,10},{6,14},... | collective-permute-start | bytes 983048 | tf_op jit(solution)/shard_map/ppermute | solution.py:31
  52.5 49.6 %collective-permute-start.8 = (bf16[2,4,4,16,1280]{4,3,2,1,0:T(8,128)(2,1)S(1)}, bf16[2,4,4,16,1280]{4,3,2,1,0:T(8,128)(2,1)S(1)}, u32[]{:S(2)}, u32[]{:S(2)}) collective-permute-start(bf16[2,4,4,16,1280]{4,3,2,1,0:T(8,128)(2,1)S(1)} %pad_maximum_fusion.9), channel_id=1, source_target_pairs={{0,16},{16,0},{1,17},{17,1},{2,18},{18,2},{3,19},{19,3},{4,20},{20... | collective-permute-start | bytes 3932168 | tf_op jit(solution)/shard_map/ppermute | solution.py:31
  56.3 31.6 %collective-permute-start.19 = (bf16[2,4,2,16,1280]{4,3,1,0,2:T(8,128)(2,1)S(1)}, bf16[2,4,2,16,1280]{4,3,1,0,2:T(8,128)(2,1)S(1)}, u32[]{:S(2)}, u32[]{:S(2)}) collective-permute-start(bf16[2,4,2,16,1280]{4,3,1,0,2:T(8,128)(2,1)S(1)} %pad_maximum_fusion.29), channel_id=1, source_target_pairs={{0,2},{1,3},{2,0},{3,1},{4,6},{5,7},{6,4},{7,5},{8,10},{9,11},{10,... | collective-permute-start | bytes 1966088 | tf_op jit(solution)/shard_map/ppermute | solution.py:31
  61.0 30.8 %collective-permute-start.5 = (bf16[128,2560]{1,0:T(8,128)(2,1)S(1)}, bf16[128,2560]{1,0:T(8,128)(2,1)S(1)}, u32[]{:S(2)}, u32[]{:S(2)}) collective-permute-start(bf16[128,2560]{1,0:T(8,128)(2,1)S(1)} %pad_maximum_fusion.27), channel_id=1, source_target_pairs={{0,4},{4,0},{8,12},{12,8},{1,5},{5,1},{9,13},{13,9},{2,6},{6,2},{1... | collective-permute-start | bytes 1966088 | tf_op jit(solution)/shard_map/ppermute | solution.py:31
  66.7 25.1 %collective-permute-start.50 = (bf16[128,2560]{1,0:T(8,128)(2,1)S(1)}, bf16[128,2560]{1,0:T(8,128)(2,1)S(1)}, u32[]{:S(2)}, u32[]{:S(2)}) collective-permute-start(bf16[128,2560]{1,0:T(8,128)(2,1)S(1)} %pad_maximum_fusion.32), channel_id=1, source_target_pairs={{0,4},{4,0},{8,12},{12,8},{1,5},{5,1},{9,13},{13,9},{2,6},{6,2},{1... | collective-permute-start | bytes 1966088 | tf_op jit(solution)/shard_map/ppermute | solution.py:31
  88.8 44.9 %collective-permute-start.20 = (bf16[2,4,4,16,1280]{4,3,1,0,2:T(8,128)(2,1)}, bf16[2,4,4,16,1280]{4,3,1,0,2:T(8,128)(2,1)S(1)}, u32[]{:S(2)}, u32[]{:S(2)}) collective-permute-start(bf16[2,4,4,16,1280]{4,3,1,0,2:T(8,128)(2,1)} %constant_dynamic-update-slice_fusion), channel_id=1, source_target_pairs={{0,16},{16,0},{1,17},{17,1},{2,18},{18,2},{3,19},{19,3},{4,20},{20... | collective-permute-start | bytes 3932168 | tf_op jit(solution)/shard_map/ppermute | solution.py:31
  98.9 31.3 %collective-permute-start.31 = (bf16[2,4,2,16,1280]{4,3,1,0,2:T(8,128)(2,1)S(1)}, bf16[2,4,2,16,1280]{4,3,1,0,2:T(8,128)(2,1)S(1)}, u32[]{:S(2)}, u32[]{:S(2)}) collective-permute-start(bf16[2,4,2,16,1280]{4,3,1,0,2:T(8,128)(2,1)S(1)} %pad_maximum_fusion.30), channel_id=1, source_target_pairs={{0,2},{1,3},{2,0},{3,1},{4,6},{5,7},{6,4},{7,5},{8,10},{9,11},{10,... | collective-permute-start | bytes 1966088 | tf_op jit(solution)/shard_map/ppermute | solution.py:31
  114.3 28.7 %collective-permute-start.9 = (bf16[224,2560]{1,0:T(8,128)(2,1)S(1)}, bf16[224,2560]{1,0:T(8,128)(2,1)S(1)}, u32[]{:S(2)}, u32[]{:S(2)}) collective-permute-start(bf16[224,2560]{1,0:T(8,128)(2,1)S(1)} %slice.565), channel_id=1, source_target_pairs={{0,4},{4,0},{8,12},{12,8},{1,5},{5,1},{9,13},{13,9},{2,6},{6,2},{1... | collective-permute-start | bytes 3440648 | tf_op jit(solution)/shard_map/ppermute | solution.py:31
  133.1 53.6 %collective-permute-start.32 = (bf16[2,4,4,16,1280]{4,3,1,0,2:T(8,128)(2,1)}, bf16[2,4,4,16,1280]{4,3,1,0,2:T(8,128)(2,1)}, u32[]{:S(2)}, u32[]{:S(2)}) collective-permute-start(bf16[2,4,4,16,1280]{4,3,1,0,2:T(8,128)(2,1)} %constant_dynamic-update-slice_fusion.3), channel_id=1, source_target_pairs={{0,16},{16,0},{1,17},{17,1},{2,18},{18,2},{3,19},{19,3},{4,20},{20... | collective-permute-start | bytes 3932168 | tf_op jit(solution)/shard_map/ppermute | solution.py:31
  139.8 45.2 %collective-permute-start.43 = (bf16[2,4,2,16,1280]{4,3,1,0,2:T(8,128)(2,1)S(1)}, bf16[2,4,2,16,1280]{4,3,1,0,2:T(8,128)(2,1)S(1)}, u32[]{:S(2)}, u32[]{:S(2)}) collective-permute-start(bf16[2,4,2,16,1280]{4,3,1,0,2:T(8,128)(2,1)S(1)} %pad_maximum_fusion.31), channel_id=1, source_target_pairs={{0,2},{1,3},{2,0},{3,1},{4,6},{5,7},{6,4},{7,5},{8,10},{9,11},{10,... | collective-permute-start | bytes 1966088 | tf_op jit(solution)/shard_map/ppermute | solution.py:31
  155.2 16.0 %collective-permute-start.10 = (bf16[112,2560]{1,0:T(8,128)(2,1)S(1)}, bf16[112,2560]{1,0:T(8,128)(2,1)S(1)}, u32[]{:S(2)}, u32[]{:S(2)}) collective-permute-start(bf16[112,2560]{1,0:T(8,128)(2,1)S(1)} %slice.575), channel_id=1, source_target_pairs={{0,8},{4,12},{8,0},{12,4},{1,9},{5,13},{9,1},{13,5},{2,10},{6,14},... | collective-permute-start | bytes 1720328 | tf_op jit(solution)/shard_map/ppermute | solution.py:31
  156.8 25.0 %collective-permute-start.12 = (bf16[112,2560]{1,0:T(8,128)(2,1)}, bf16[112,2560]{1,0:T(8,128)(2,1)S(1)}, u32[]{:S(2)}, u32[]{:S(2)}) collective-permute-start(bf16[112,2560]{1,0:T(8,128)(2,1)} %slice.574), channel_id=1, source_target_pairs={{0,8},{4,12},{8,0},{12,4},{1,9},{5,13},{9,1},{13,5},{2,10},{6,14},... | collective-permute-start | bytes 1720328 | tf_op jit(solution)/shard_map/ppermute | solution.py:31
  157.4 43.1 %collective-permute-start.21 = (bf16[224,2560]{1,0:T(8,128)(2,1)S(1)}, bf16[224,2560]{1,0:T(8,128)(2,1)S(1)}, u32[]{:S(2)}, u32[]{:S(2)}) collective-permute-start(bf16[224,2560]{1,0:T(8,128)(2,1)S(1)} %slice.563), channel_id=1, source_target_pairs={{0,4},{4,0},{8,12},{12,8},{1,5},{5,1},{9,13},{13,9},{2,6},{6,2},{1... | collective-permute-start | bytes 3440648 | tf_op jit(solution)/shard_map/ppermute | solution.py:31
  171.2 30.5 %collective-permute-start.23 = (bf16[224,2560]{1,0:T(8,128)(2,1)S(1)}, bf16[224,2560]{1,0:T(8,128)(2,1)S(1)}, u32[]{:S(2)}, u32[]{:S(2)}) collective-permute-start(bf16[224,2560]{1,0:T(8,128)(2,1)S(1)} %slice.562), channel_id=1, source_target_pairs={{0,4},{4,0},{8,12},{12,8},{1,5},{5,1},{9,13},{13,9},{2,6},{6,2},{1... | collective-permute-start | bytes 3440648 | tf_op jit(solution)/shard_map/ppermute | solution.py:31
  183.5 15.9 %collective-permute-start.13 = (bf16[112,2560]{1,0:T(8,128)(2,1)S(1)}, bf16[112,2560]{1,0:T(8,128)(2,1)S(1)}, u32[]{:S(2)}, u32[]{:S(2)}) collective-permute-start(bf16[112,2560]{1,0:T(8,128)(2,1)S(1)} %get-tuple-element.48), channel_id=1, source_target_pairs={{0,8},{4,12},{8,0},{12,4},{1,9},{5,13},{9,1},{13,5},{2,10},{6,14},... | collective-permute-start | bytes 1720328 | tf_op jit(solution)/shard_map/ppermute | solution.py:31
  186.1 37.6 %collective-permute-start.44 = (bf16[2,4,4,16,1280]{4,3,1,0,2:T(8,128)(2,1)}, bf16[2,4,4,16,1280]{4,3,1,0,2:T(8,128)(2,1)}, u32[]{:S(2)}, u32[]{:S(2)}) collective-permute-start(bf16[2,4,4,16,1280]{4,3,1,0,2:T(8,128)(2,1)} %pad_maximum_fusion.10), channel_id=1, source_target_pairs={{0,16},{16,0},{1,17},{17,1},{2,18},{18,2},{3,19},{19,3},{4,20},{20... | collective-permute-start | bytes 3932168 | tf_op jit(solution)/shard_map/ppermute | solution.py:31
  186.7 28.5 %collective-permute-start.51 = (bf16[112,2560]{1,0:T(8,128)(2,1)}, bf16[112,2560]{1,0:T(8,128)(2,1)S(1)}, u32[]{:S(2)}, u32[]{:S(2)}) collective-permute-start(bf16[112,2560]{1,0:T(8,128)(2,1)} %get-tuple-element.56), channel_id=1, source_target_pairs={{0,8},{4,12},{8,0},{12,4},{1,9},{5,13},{9,1},{13,5},{2,10},{6,14},... | collective-permute-start | bytes 1720328 | tf_op jit(solution)/shard_map/ppermute | solution.py:31
  200.6 25.5 %collective-permute-start.14 = (bf16[224,2560]{1,0:T(8,128)(2,1)}, bf16[224,2560]{1,0:T(8,128)(2,1)S(1)}, u32[]{:S(2)}, u32[]{:S(2)}) collective-permute-start(bf16[224,2560]{1,0:T(8,128)(2,1)} %pad_maximum_fusion.13), channel_id=1, source_target_pairs={{0,4},{4,0},{8,12},{12,8},{1,5},{5,1},{9,13},{13,9},{2,6},{6,2},{1... | collective-permute-start | bytes 3440648 | tf_op jit(solution)/shard_map/ppermute | solution.py:31
  217.3 24.4 %collective-permute-start.52 = (bf16[224,2560]{1,0:T(8,128)(2,1)}, bf16[224,2560]{1,0:T(8,128)(2,1)}, u32[]{:S(2)}, u32[]{:S(2)}) collective-permute-start(bf16[224,2560]{1,0:T(8,128)(2,1)} %pad_maximum_fusion.16), channel_id=1, source_target_pairs={{0,4},{4,0},{8,12},{12,8},{1,5},{5,1},{9,13},{13,9},{2,6},{6,2},{1... | collective-permute-start | bytes 3440648 | tf_op jit(solution)/shard_map/ppermute | solution.py:31
  217.8 26.8 %collective-permute-start.22 = (bf16[112,2560]{1,0:T(8,128)(2,1)}, bf16[112,2560]{1,0:T(8,128)(2,1)}, u32[]{:S(2)}, u32[]{:S(2)}) collective-permute-start(bf16[112,2560]{1,0:T(8,128)(2,1)} %slice.573), channel_id=1, source_target_pairs={{0,8},{4,12},{8,0},{12,4},{1,9},{5,13},{9,1},{13,5},{2,10},{6,14},... | collective-permute-start | bytes 1720328 | tf_op jit(solution)/shard_map/ppermute | solution.py:31
  220.5 15.8 %collective-permute-start.33 = (bf16[224,2560]{1,0:T(8,128)(2,1)}, bf16[224,2560]{1,0:T(8,128)(2,1)}, u32[]{:S(2)}, u32[]{:S(2)}) collective-permute-start(bf16[224,2560]{1,0:T(8,128)(2,1)} %slice.561), channel_id=1, source_target_pairs={{0,4},{4,0},{8,12},{12,8},{1,5},{5,1},{9,13},{13,9},{2,6},{6,2},{1... | collective-permute-start | bytes 3440648 | tf_op jit(solution)/shard_map/ppermute | solution.py:31
  223.7 22.6 %collective-permute-start.24 = (bf16[112,2560]{1,0:T(8,128)(2,1)}, bf16[112,2560]{1,0:T(8,128)(2,1)}, u32[]{:S(2)}, u32[]{:S(2)}) collective-permute-start(bf16[112,2560]{1,0:T(8,128)(2,1)} %slice.572), channel_id=1, source_target_pairs={{0,8},{4,12},{8,0},{12,4},{1,9},{5,13},{9,1},{13,5},{2,10},{6,14},... | collective-permute-start | bytes 1720328 | tf_op jit(solution)/shard_map/ppermute | solution.py:31
  237.9 20.6 %collective-permute-start.34 = (bf16[112,2560]{1,0:T(8,128)(2,1)S(1)}, bf16[112,2560]{1,0:T(8,128)(2,1)S(1)}, u32[]{:S(2)}, u32[]{:S(2)}) collective-permute-start(bf16[112,2560]{1,0:T(8,128)(2,1)S(1)} %slice.571), channel_id=1, source_target_pairs={{0,8},{4,12},{8,0},{12,4},{1,9},{5,13},{9,1},{13,5},{2,10},{6,14},... | collective-permute-start | bytes 1720328 | tf_op jit(solution)/shard_map/ppermute | solution.py:31
  241.1 28.7 %collective-permute-start.36 = (bf16[112,2560]{1,0:T(8,128)(2,1)S(1)}, bf16[112,2560]{1,0:T(8,128)(2,1)S(1)}, u32[]{:S(2)}, u32[]{:S(2)}) collective-permute-start(bf16[112,2560]{1,0:T(8,128)(2,1)S(1)} %slice.570), channel_id=1, source_target_pairs={{0,8},{4,12},{8,0},{12,4},{1,9},{5,13},{9,1},{13,5},{2,10},{6,14},... | collective-permute-start | bytes 1720328 | tf_op jit(solution)/shard_map/ppermute | solution.py:31
  241.8 44.5 %collective-permute-start.15 = (bf16[4,4,16,1280]{3,2,0,1:T(8,128)(2,1)}, bf16[4,4,16,1280]{3,2,0,1:T(8,128)(2,1)S(1)}, u32[]{:S(2)}, u32[]{:S(2)}) collective-permute-start(bf16[4,4,16,1280]{3,2,0,1:T(8,128)(2,1)} %copy.48), channel_id=1, source_target_pairs={{0,16},{16,0},{1,17},{17,1},{2,18},{18,2},{3,19},{19,3},{4,20},{20... | collective-permute-start | bytes 1966088 | tf_op jit(solution)/shard_map/ppermute | solution.py:31
  273.2 54.5 %collective-permute-start.53 = (bf16[112,2560]{1,0:T(8,128)(2,1)S(1)}, bf16[112,2560]{1,0:T(8,128)(2,1)S(1)}, u32[]{:S(2)}, u32[]{:S(2)}) collective-permute-start(bf16[112,2560]{1,0:T(8,128)(2,1)S(1)} %get-tuple-element.90), channel_id=1, source_target_pairs={{0,8},{4,12},{8,0},{12,4},{1,9},{5,13},{9,1},{13,5},{2,10},{6,14},... | collective-permute-start | bytes 1720328 | tf_op jit(solution)/shard_map/ppermute | solution.py:31
  274.7 51.8 %collective-permute-start.25 = (bf16[112,2560]{1,0:T(8,128)(2,1)S(1)}, bf16[112,2560]{1,0:T(8,128)(2,1)S(1)}, u32[]{:S(2)}, u32[]{:S(2)}) collective-permute-start(bf16[112,2560]{1,0:T(8,128)(2,1)S(1)} %get-tuple-element.92), channel_id=1, source_target_pairs={{0,8},{4,12},{8,0},{12,4},{1,9},{5,13},{9,1},{13,5},{2,10},{6,14},... | collective-permute-start | bytes 1720328 | tf_op jit(solution)/shard_map/ppermute | solution.py:31
  287.9 16.2 %collective-permute-start.16 = (bf16[4,2,16,1280]{3,2,0,1:T(8,128)(2,1)S(1)}, bf16[4,2,16,1280]{3,2,0,1:T(8,128)(2,1)S(1)}, u32[]{:S(2)}, u32[]{:S(2)}) collective-permute-start(bf16[4,2,16,1280]{3,2,0,1:T(8,128)(2,1)S(1)} %slice.579), channel_id=1, source_target_pairs={{0,2},{1,3},{2,0},{3,1},{4,6},{5,7},{6,4},{7,5},{8,10},{9,11},{10,... | collective-permute-start | bytes 983048 | tf_op jit(solution)/shard_map/ppermute | solution.py:31
  289.5 24.2 %collective-permute-start.60 = (bf16[112,2560]{1,0:T(8,128)(2,1)S(1)}, bf16[112,2560]{1,0:T(8,128)(2,1)S(1)}, u32[]{:S(2)}, u32[]{:S(2)}) collective-permute-start(bf16[112,2560]{1,0:T(8,128)(2,1)S(1)} %get-tuple-element.34), channel_id=1, source_target_pairs={{0,8},{4,12},{8,0},{12,4},{1,9},{5,13},{9,1},{13,5},{2,10},{6,14},... | collective-permute-start | bytes 1720328 | tf_op jit(solution)/shard_map/ppermute | solution.py:31
  290.9 33.1 %collective-permute-start.37 = (bf16[112,2560]{1,0:T(8,128)(2,1)S(1)}, bf16[112,2560]{1,0:T(8,128)(2,1)S(1)}, u32[]{:S(2)}, u32[]{:S(2)}) collective-permute-start(bf16[112,2560]{1,0:T(8,128)(2,1)S(1)} %get-tuple-element.52), channel_id=1, source_target_pairs={{0,8},{4,12},{8,0},{12,4},{1,9},{5,13},{9,1},{13,5},{2,10},{6,14},... | collective-permute-start | bytes 1720328 | tf_op jit(solution)/shard_map/ppermute | solution.py:31
  304.1 27.8 %collective-permute-start.45 = (bf16[224,2560]{1,0:T(8,128)(2,1)S(1)}, bf16[224,2560]{1,0:T(8,128)(2,1)S(1)}, u32[]{:S(2)}, u32[]{:S(2)}) collective-permute-start(bf16[224,2560]{1,0:T(8,128)(2,1)S(1)} %slice.559), channel_id=1, source_target_pairs={{0,4},{4,0},{8,12},{12,8},{1,5},{5,1},{9,13},{13,9},{2,6},{6,2},{1... | collective-permute-start | bytes 3440648 | tf_op jit(solution)/shard_map/ppermute | solution.py:31
  313.7 20.0 %collective-permute-start.47 = (bf16[224,2560]{1,0:T(8,128)(2,1)S(1)}, bf16[224,2560]{1,0:T(8,128)(2,1)S(1)}, u32[]{:S(2)}, u32[]{:S(2)}) collective-permute-start(bf16[224,2560]{1,0:T(8,128)(2,1)S(1)} %slice.558), channel_id=1, source_target_pairs={{0,4},{4,0},{8,12},{12,8},{1,5},{5,1},{9,13},{13,9},{2,6},{6,2},{1... | collective-permute-start | bytes 3440648 | tf_op jit(solution)/shard_map/ppermute | solution.py:31
  327.7 16.6 %collective-permute-start.26 = (bf16[224,2560]{1,0:T(8,128)(2,1)}, bf16[224,2560]{1,0:T(8,128)(2,1)}, u32[]{:S(2)}, u32[]{:S(2)}) collective-permute-start(bf16[224,2560]{1,0:T(8,128)(2,1)} %pad_maximum_fusion.14), channel_id=1, source_target_pairs={{0,4},{4,0},{8,12},{12,8},{1,5},{5,1},{9,13},{13,9},{2,6},{6,2},{1... | collective-permute-start | bytes 3440648 | tf_op jit(solution)/shard_map/ppermute | solution.py:31
  331.9 28.7 %collective-permute-start.54 = (bf16[224,2560]{1,0:T(8,128)(2,1)}, bf16[224,2560]{1,0:T(8,128)(2,1)}, u32[]{:S(2)}, u32[]{:S(2)}) collective-permute-start(bf16[224,2560]{1,0:T(8,128)(2,1)} %pad_maximum_fusion.17), channel_id=1, source_target_pairs={{0,4},{4,0},{8,12},{12,8},{1,5},{5,1},{9,13},{13,9},{2,6},{6,2},{1... | collective-permute-start | bytes 3440648 | tf_op jit(solution)/shard_map/ppermute | solution.py:31
  332.0 47.3 %collective-permute-start.61 = (bf16[224,2560]{1,0:T(8,128)(2,1)}, bf16[224,2560]{1,0:T(8,128)(2,1)}, u32[]{:S(2)}, u32[]{:S(2)}) collective-permute-start(bf16[224,2560]{1,0:T(8,128)(2,1)} %pad_maximum_fusion.19), channel_id=1, source_target_pairs={{0,4},{4,0},{8,12},{12,8},{1,5},{5,1},{9,13},{13,9},{2,6},{6,2},{1... | collective-permute-start | bytes 3440648 | tf_op jit(solution)/shard_map/ppermute | solution.py:31
  333.7 48.0 %collective-permute-start.46 = (bf16[112,2560]{1,0:T(8,128)(2,1)}, bf16[112,2560]{1,0:T(8,128)(2,1)}, u32[]{:S(2)}, u32[]{:S(2)}) collective-permute-start(bf16[112,2560]{1,0:T(8,128)(2,1)} %slice.569), channel_id=1, source_target_pairs={{0,8},{4,12},{8,0},{12,4},{1,9},{5,13},{9,1},{13,5},{2,10},{6,14},... | collective-permute-start | bytes 1720328 | tf_op jit(solution)/shard_map/ppermute | solution.py:31
  336.4 40.4 %collective-permute-start.48 = (bf16[112,2560]{1,0:T(8,128)(2,1)}, bf16[112,2560]{1,0:T(8,128)(2,1)}, u32[]{:S(2)}, u32[]{:S(2)}) collective-permute-start(bf16[112,2560]{1,0:T(8,128)(2,1)} %slice.568), channel_id=1, source_target_pairs={{0,8},{4,12},{8,0},{12,4},{1,9},{5,13},{9,1},{13,5},{2,10},{6,14},... | collective-permute-start | bytes 1720328 | tf_op jit(solution)/shard_map/ppermute | solution.py:31
  344.2 68.0 %collective-permute-start.39 = (bf16[4,4,16,1280]{3,2,0,1:T(8,128)(2,1)}, bf16[4,4,16,1280]{3,2,0,1:T(8,128)(2,1)S(1)}, u32[]{:S(2)}, u32[]{:S(2)}) collective-permute-start(bf16[4,4,16,1280]{3,2,0,1:T(8,128)(2,1)} %copy.46), channel_id=1, source_target_pairs={{0,16},{16,0},{1,17},{17,1},{2,18},{18,2},{3,19},{19,3},{4,20},{20... | collective-permute-start | bytes 1966088 | tf_op jit(solution)/shard_map/ppermute | solution.py:31
  384.2 26.5 %collective-permute-start.62 = (bf16[112,2560]{1,0:T(8,128)(2,1)S(1)}, bf16[112,2560]{1,0:T(8,128)(2,1)S(1)}, u32[]{:S(2)}, u32[]{:S(2)}) collective-permute-start(bf16[112,2560]{1,0:T(8,128)(2,1)S(1)} %get-tuple-element.32), channel_id=1, source_target_pairs={{0,8},{4,12},{8,0},{12,4},{1,9},{5,13},{9,1},{13,5},{2,10},{6,14},... | collective-permute-start | bytes 1720328 | tf_op jit(solution)/shard_map/ppermute | solution.py:31
  385.7 24.9 %collective-permute-start.55 = (bf16[112,2560]{1,0:T(8,128)(2,1)S(1)}, bf16[112,2560]{1,0:T(8,128)(2,1)S(1)}, u32[]{:S(2)}, u32[]{:S(2)}) collective-permute-start(bf16[112,2560]{1,0:T(8,128)(2,1)S(1)} %get-tuple-element.72), channel_id=1, source_target_pairs={{0,8},{4,12},{8,0},{12,4},{1,9},{5,13},{9,1},{13,5},{2,10},{6,14},... | collective-permute-start | bytes 1720328 | tf_op jit(solution)/shard_map/ppermute | solution.py:31
  392.8 20.1 %collective-permute-start.27 = (bf16[4,4,16,1280]{3,2,0,1:T(8,128)(2,1)S(1)}, bf16[4,4,16,1280]{3,2,0,1:T(8,128)(2,1)S(1)}, u32[]{:S(2)}, u32[]{:S(2)}) collective-permute-start(bf16[4,4,16,1280]{3,2,0,1:T(8,128)(2,1)S(1)} %copy.47), channel_id=1, source_target_pairs={{0,16},{16,0},{1,17},{17,1},{2,18},{18,2},{3,19},{19,3},{4,20},{20... | collective-permute-start | bytes 1966088 | tf_op jit(solution)/shard_map/ppermute | solution.py:31
  410.6 47.7 %collective-permute-start.56 = (bf16[224,2560]{1,0:T(8,128)(2,1)S(1)}, bf16[224,2560]{1,0:T(8,128)(2,1)S(1)}, u32[]{:S(2)}, u32[]{:S(2)}) collective-permute-start(bf16[224,2560]{1,0:T(8,128)(2,1)S(1)} %pad_maximum_fusion.18), channel_id=1, source_target_pairs={{0,4},{4,0},{8,12},{12,8},{1,5},{5,1},{9,13},{13,9},{2,6},{6,2},{1... | collective-permute-start | bytes 3440648 | tf_op jit(solution)/shard_map/ppermute | solution.py:31
  410.8 65.8 %collective-permute-start.63 = (bf16[224,2560]{1,0:T(8,128)(2,1)S(1)}, bf16[224,2560]{1,0:T(8,128)(2,1)S(1)}, u32[]{:S(2)}, u32[]{:S(2)}) collective-permute-start(bf16[224,2560]{1,0:T(8,128)(2,1)S(1)} %pad_maximum_fusion.20), channel_id=1, source_target_pairs={{0,4},{4,0},{8,12},{12,8},{1,5},{5,1},{9,13},{13,9},{2,6},{6,2},{1... | collective-permute-start | bytes 3440648 | tf_op jit(solution)/shard_map/ppermute | solution.py:31
  412.5 25.6 %collective-permute-start.40 = (bf16[4,2,16,1280]{3,2,0,1:T(8,128)(2,1)S(1)}, bf16[4,2,16,1280]{3,2,0,1:T(8,128)(2,1)S(1)}, u32[]{:S(2)}, u32[]{:S(2)}) collective-permute-start(bf16[4,2,16,1280]{3,2,0,1:T(8,128)(2,1)S(1)} %slice.577), channel_id=1, source_target_pairs={{0,2},{1,3},{2,0},{3,1},{4,6},{5,7},{6,4},{7,5},{8,10},{9,11},{10,... | collective-permute-start | bytes 983048 | tf_op jit(solution)/shard_map/ppermute | solution.py:31
  413.2 31.1 %collective-permute-start.28 = (bf16[4,2,16,1280]{3,2,0,1:T(8,128)(2,1)S(1)}, bf16[4,2,16,1280]{3,2,0,1:T(8,128)(2,1)S(1)}, u32[]{:S(2)}, u32[]{:S(2)}) collective-permute-start(bf16[4,2,16,1280]{3,2,0,1:T(8,128)(2,1)S(1)} %slice.578), channel_id=1, source_target_pairs={{0,2},{1,3},{2,0},{3,1},{4,6},{5,7},{6,4},{7,5},{8,10},{9,11},{10,... | collective-permute-start | bytes 983048 | tf_op jit(solution)/shard_map/ppermute | solution.py:31
  461.6 16.7 %collective-permute-start.57 = (bf16[4,4,16,1280]{3,2,0,1:T(8,128)(2,1)S(1)}, bf16[4,4,16,1280]{3,2,0,1:T(8,128)(2,1)S(1)}, u32[]{:S(2)}, u32[]{:S(2)}) collective-permute-start(bf16[4,4,16,1280]{3,2,0,1:T(8,128)(2,1)S(1)} %copy.45), channel_id=1, source_target_pairs={{0,16},{16,0},{1,17},{17,1},{2,18},{18,2},{3,19},{19,3},{4,20},{20... | collective-permute-start | bytes 1966088 | tf_op jit(solution)/shard_map/ppermute | solution.py:31
  (46 other events, 511.2 us)

commit v2 on v0

v2 whole, which is shorter than its diff:
```python
import jax
import jax.numpy as jnp
from jax import lax
from jax.sharding import PartitionSpec as P

CHUNKS = (None, (0, 2), (2, 4), (4, 6), (6, 8))
GROUPS = ((0, 1, 2), (3, 4))


def gelu_pair(preact):
    normal_cdf = 0.5 * (1.0 + lax.erf(preact * 0.7071067811865476))
    normal_pdf = jnp.exp(-0.5 * preact * preact) * 0.3989422804014327
    return (preact * normal_cdf, normal_cdf + preact * normal_pdf)


def times_transpose(left_rows, matrix):
    return lax.dot_general(
        left_rows, matrix, (((1,), (1,)), ((), ())), preferred_element_type=jnp.float32
    )


def over_tokens(left_rows, right_rows):
    return lax.dot_general(
        left_rows, right_rows, (((0,), (0,)), ((), ())), preferred_element_type=jnp.float32
    )


def swap(array, bit, axis="col"):
    pairs = [(i, i ^ bit) for i in range(lax.axis_size(axis))]
    return lax.ppermute(array, axis, pairs)


def steps():
    return [
        (1 << k, axis) for axis in ("depth", "row") for k in range(lax.axis_size(axis).bit_length() - 1)
    ]


def quarter(array, index):
    rows = array.shape[0] // 4
    return lax.dynamic_slice_in_dim(array, index * rows, rows, 0)


def body(tokens, w_up, bias_up, w_down, cotangent):
    me = lax.axis_index("col")
    rows, width = tokens.shape
    fourth = rows // 4
    exchanges = steps()
    last_step = len(exchanges) - 1
    last = len(CHUNKS) - 1

    def relative(array):
        return jnp.stack([quarter(array, me ^ j) for j in (0, 2, 1, 3)])

    def joined(*arrays, axis=0):
        return jnp.concatenate(arrays, axis=axis)

    state = {"local": jnp.stack([relative(tokens), relative(cotangent)]), "weights": (w_up, w_down)}

    def gather(i, first, final):
        for step in range(first, final + 1):
            if step == 0:
                low, high = CHUNKS[i]
                block = state["local"][:, :, None, fourth * low // 8 : fourth * high // 8]
            else:
                block = joined(*state["gather", i], axis=2)
            state["gather", i] = (block, swap(block, *exchanges[step]))

    def z1(i):
        gather(i, 0, 0)

    def z2(i):
        gather(i, 1, last_step - 1)

    def y(i):
        gather(i, last_step, last_step)

    def forward(i):
        if CHUNKS[i] is None:
            stacked = state["local"]
        else:
            block, got = state.pop(("gather", i))
            stacked = joined(block[:, :, 1:], got, axis=2)
        token_rows, cotan_rows = stacked.reshape(2, -1, width)
        state["rows", i] = (token_rows, cotan_rows)
        up, down = state["weights"]
        half = token_rows.shape[0] // 2
        state["sums", i] = tuple(
            (part[:half], part[half:].astype(jnp.bfloat16))
            for part in (
                jnp.dot(token_rows, up, preferred_element_type=jnp.float32),
                times_transpose(cotan_rows, down),
            )
        )

    def over_cores(i):
        state["sums", i] = tuple((mine, swap(send, 1)) for mine, send in state["sums", i])

    def over_chips(i):
        pairs = []
        for mine, got in state["sums", i]:
            total = mine + got.astype(jnp.float32)
            half = total.shape[0] // 2
            pairs.append((total[:half], swap(total[half:].astype(jnp.bfloat16), 2)))
        state["sums", i] = tuple(pairs)

    def spread_chips(i):
        preact, back = (mine + got.astype(jnp.float32) for mine, got in state.pop(("sums", i)))
        value, derivative = gelu_pair(preact + bias_up)
        pair = ((back * derivative).astype(jnp.bfloat16), value.astype(jnp.bfloat16))
        state["pair", i] = tuple((part, swap(part, 2)) for part in pair)

    def spread_cores(i):
        halves = [joined(*pair) for pair in state["pair", i]]
        state["pair", i] = tuple((half, swap(half, 1)) for half in halves)

    def backward(i):
        hidden, activated = (joined(*pair) for pair in state.pop(("pair", i)))
        state["hidden", i], state["activated", i] = hidden, activated
        part = times_transpose(hidden, state["weights"][0])
        if CHUNKS[i] is None:
            state["total", i] = part.reshape(4, fourth, width)
        else:
            low, high = CHUNKS[i]
            part = part.reshape(4, -1, fourth * high // 8 - fourth * low // 8, width)
            half = (part.shape[1] + 1) // 2
            state["part", i] = (part[:, : half - 1], part[:, half - 1 :].astype(jnp.bfloat16))

    def ry(i):
        keep, send = state["part", i]
        state["part", i] = (keep, swap(send, *exchanges[last_step]))

    def scatter(i, step):
        keep, got = state["part", i]
        got = got.astype(jnp.float32)
        if step == last_step - 1:
            total = joined(got[:, :1], got[:, 1:] + keep, axis=1)
        else:
            total = keep + got
        half = total.shape[1] // 2
        kind = jnp.bfloat16 if half > 1 else jnp.float32
        state["part", i] = (total[:, :half], swap(total[:, half:].astype(kind), *exchanges[step]))

    def rz2(i):
        for step in range(last_step - 1, 0, -1):
            scatter(i, step)

    def rz1(i):
        scatter(i, 0)

    def weight_grad(name, other, which, flip):
        left, right = (
            joined(*(state[key, i][k] if key == "rows" else state[key, i] for i in GROUPS[which]))
            for key, k in ((("rows", 0), (other, None)) if not flip else ((other, None), ("rows", 1)))
        )
        grad = over_tokens(left, right), jnp.sum(right, axis=0, dtype=jnp.float32)
        if which > 0:
            grad = tuple(new + old for new, old in zip(grad, state[name]))
        state[name] = grad

    def up(which):
        weight_grad("up", "hidden", which, False)

    def down(which):
        weight_grad("down", "activated", which, True)

    phases = (
        ((forward, 0), (over_cores, 0), (z1, 1)),
        ((over_chips, 0), (z2, 1), (z1, 2)),
        ((spread_chips, 0), (y, 1), (z2, 2)),
        ((forward, 1), (over_cores, 1), (spread_cores, 0), (y, 2), (z1, 3)),
        ((over_chips, 1), (forward, 2), (z2, 3), (backward, 0)),
        ((spread_chips, 1), (over_cores, 2), (y, 3), (z1, 4)),
        ((over_chips, 2), (forward, 3), (z2, 4), (spread_cores, 1)),
        ((spread_chips, 2), (over_cores, 3), (y, 4)),
        ((over_chips, 3), (forward, 4), (spread_cores, 2), (backward, 1)),
        ((spread_chips, 3), (over_cores, 4), (ry, 1)),
        ((over_chips, 4), (spread_cores, 3), (backward, 2), (rz2, 1), (up, 0)),
        ((spread_chips, 4), (backward, 3), (ry, 2), (rz1, 1), (down, 0)),
        ((spread_cores, 4), (backward, 4), (ry, 3), (rz2, 2)),
        ((ry, 4), (rz2, 3), (rz1, 2), (up, 1)),
        ((rz2, 4), (rz1, 3), (down, 1)),
        ((rz1, 4),),
    )
    for phase in phases:
        for work, i in phase:
            work(i)
        keys = list(state)
        values = lax.optimization_barrier(tuple(state[key] for key in keys))
        state = dict(zip(keys, values))

    (up_grad, up_bias_grad), (down_grad, down_bias_grad) = state["up"], state["down"]
    others = [sum(state["part", i]).reshape(4, -1, width) for i in range(1, last + 1)]
    input_grad = (state["total", 0] + joined(*others, axis=1)).astype(jnp.bfloat16)
    input_grad = input_grad.reshape(rows, width)
    input_grad = joined(*(quarter(input_grad, (2 * (j & 1)) | (j >> 1)) for j in [me ^ q for q in range(4)]))
    return (input_grad, up_grad, up_bias_grad, down_grad, down_bias_grad)


def solution(mesh):
    return jax.shard_map(
        body,
        mesh=mesh,
        in_specs=(
            P(("row", "depth"), "col"),
            P("col", ("row", "depth")),
            P(("row", "depth")),
            P(("row", "depth"), "col"),
            P(("row", "depth"), "col"),
        ),
        out_specs=(
            P(("row", "depth"), "col"),
            P("col", ("row", "depth")),
            P(("row", "depth")),
            P(("row", "depth"), "col"),
            P("col"),
        ),
        check_vma=False,
    )
```

time: 861 us -> 483 us (0.56); the launches traced: 861 us -> 474 us
  waiting for transfers between devices: 686 us -> 225 us
  starting transfers between devices: 0.42 us -> 55.7 us
  matrix products: 99.4 us -> 127 us
  local copies, waits for them, and re-layouts: 13.9 us -> 41.3 us
  other arithmetic: 46.7 us -> 22 us
  between operations: 14.1 us -> 3.15 us
    reduce_scatter x2 -> x0, waiting for transfers between devices: 449 us -> none  [the longest x1 287 us: body(): lax.psum_scatter(jnp.concatenate([up_rows, times_transpose(cotan_all, w_d...]
    all_gather x4 -> x0, waiting for transfers between devices: 235 us -> none  [the longest x1 90.4 us: body(): lax.all_gather(cotangent, ('row', 'depth'), axis=0, tiled=True)]
    ppermute x0 -> x64, waiting for transfers between devices: none -> 225 us  [swap(): return lax.ppermute(array, axis, pairs)]
    ppermute x0 -> x64, starting transfers between devices: none -> 55.7 us  [swap(): return lax.ppermute(array, axis, pairs)]
    concatenate x1 -> x16, other arithmetic: 27.7 us -> 6.46 us  [joined(): return jnp.concatenate(arrays, axis=axis)]
    dot_general x2 -> x4, matrix products: 39.1 us -> 51.3 us  [over_tokens(): lax.dot_general(left_rows, right_rows, (((0,), (0,)), ((), ())), preferre...]
    dot_general x2 -> x10, matrix products: 39.9 us -> 51.9 us  [times_transpose(): lax.dot_general(left_rows, matrix, (((1,), (1,)), ((), ())), preferred_el...]
    slice x0 -> x84, local copies, waits for them, and re-layouts: none -> 11.3 us  [the longest x20 6.47 us: forward(): part[:half]]
  transfers between devices with their start and end apart: 6 -> 64, of which waited for: 6 -> 32; matrix products, arithmetic and copies ran while one was open for 12% -> 30% of each run, Pallas kernels for 0% -> 0%
where the time goes in v2:
time: 483 us; the launch traced here: 474 us
  waiting for transfers between devices  225 us (47%)
  matrix products  127 us (26%)
  starting transfers between devices  55.7 us (12%)
  local copies, waits for them, and re-layouts  41.3 us (9%)
  other arithmetic  22 us (5%)
    ppermute x64, waiting for transfers between devices, swap(): return lax.ppermute(array, axis, pairs)  225 us
    ppermute x64, starting transfers between devices, swap(): return lax.ppermute(array, axis, pairs)  55.7 us
    dot_general x10, matrix products, times_transpose(): lax.dot_general(left_rows, matrix, (((1,), (1,)), ((), ())), preferred_el...  51.9 us
    dot_general x4, matrix products, over_tokens(): lax.dot_general(left_rows, right_rows, (((0,), (0,)), ((), ())), preferre...  51.3 us
    dot_general x5, matrix products, forward(): jnp.dot(token_rows, up, preferred_element_type=jnp.float32)  23.4 us
    unnamed x118, local copies, waits for them, and re-layouts  22.4 us
  transfers between devices with their start and end apart: 64, of which 32 were waited for; matrix products, arithmetic and copies ran while one was open for 30% of the time, Pallas kernels for 0%

profile of v2, /device:TPU:0, one launch (start us, length us, event | category | flops | bytes accessed | tf_op | source)
XLA Modules:
  0.0 474.0 jit_solution(9864984300339287330)
XLA Ops:
  2.3 5.0 %fusion.65 = f32[256,2560]{1,0:T(8,128)S(1)} fusion(bf16[256,1280]{1,0:T(8,128)(2,1)S(1)} %bitcast.114, bf16[1280,2560]{1,0:T(8,128)(2,1)} %param.6), kind=kOutput, calls=%fused_computation.240 | convolution fusion | flops 1677721600 | bytes 9830400 | tf_op jit(solution)/shard_map/dot_general | solution.py:91
  10.2 3.1 collective-permute-start.2
  13.4 7.8 %collective-permute-done.2 = bf16[2,4,1,16,1280]{4,3,2,1,0:T(8,128)(2,1)S(1)} collective-permute-done((bf16[2,4,1,16,1280]{4,3,2,1,0:T(8,128)(2,1)S(1)}, bf16[2,4,1,16,1280]{4,3,2,1,0:T(8,128)(2,1)S(1)}, u32[]{:S(2)}, u32[]{:S(2)}) %collective-permute-start.2) | collective-permute-done | bytes 327712 | tf_op jit(solution)/shard_map/ppermute | solution.py:30
  23.1 2.7 collective-permute-start.5
  28.7 8.4 %collective-permute-done.6 = bf16[2,4,1,16,1280]{4,3,1,0,2:T(8,128)(2,1)S(1)} collective-permute-done((bf16[2,4,1,16,1280]{4,3,1,0,2:T(8,128)(2,1)S(1)}, bf16[2,4,1,16,1280]{4,3,1,0,2:T(8,128)(2,1)S(1)}, u32[]{:S(2)}, u32[]{:S(2)}) %collective-permute-start.6) | collective-permute-done | bytes 327712 | tf_op jit(solution)/shard_map/ppermute | solution.py:30
  37.2 4.1 collective-permute-done.4
  41.3 12.4 %collective-permute-done.5 = bf16[2,4,2,16,1280]{4,3,2,1,0:T(8,128)(2,1)S(1)} collective-permute-done((bf16[2,4,2,16,1280]{4,3,2,1,0:T(8,128)(2,1)S(1)}, bf16[2,4,2,16,1280]{4,3,2,1,0:T(8,128)(2,1)S(1)}, u32[]{:S(2)}, u32[]{:S(2)}) %collective-permute-start.5) | collective-permute-done | bytes 655392 | tf_op jit(solution)/shard_map/ppermute | solution.py:30
  58.1 8.6 %collective-permute-done.10 = bf16[64,2560]{1,0:T(8,128)(2,1)S(1)} collective-permute-done((bf16[64,2560]{1,0:T(8,128)(2,1)S(1)}, bf16[64,2560]{1,0:T(8,128)(2,1)S(1)}, u32[]{:S(2)}, u32[]{:S(2)}) %collective-permute-start.10) | collective-permute-done | bytes 327712 | tf_op jit(solution)/shard_map/ppermute | solution.py:30
  66.7 3.7 collective-permute-done.9
  70.4 14.2 %collective-permute-done.8 = bf16[2,4,2,16,1280]{4,3,1,0,2:T(8,128)(2,1)S(1)} collective-permute-done((bf16[2,4,2,16,1280]{4,3,1,0,2:T(8,128)(2,1)S(1)}, bf16[2,4,2,16,1280]{4,3,1,0,2:T(8,128)(2,1)S(1)}, u32[]{:S(2)}, u32[]{:S(2)}) %collective-permute-start.8) | collective-permute-done | bytes 655392 | tf_op jit(solution)/shard_map/ppermute | solution.py:30
  86.5 3.1 fusion.67
  89.9 3.2 fusion.68
  98.1 17.8 %collective-permute-done.11 = bf16[2,4,4,16,1280]{4,3,1,0,2:T(8,128)(2,1)S(1)} collective-permute-done((bf16[2,4,4,16,1280]{4,3,1,0,2:T(8,128)(2,1)S(1)}, bf16[2,4,4,16,1280]{4,3,1,0,2:T(8,128)(2,1)S(1)}, u32[]{:S(2)}, u32[]{:S(2)}) %collective-permute-start.11) | collective-permute-done | bytes 1310752 | tf_op jit(solution)/shard_map/ppermute | solution.py:30
  122.7 3.4 fusion.69
  128.3 5.4 %fusion.70 = f32[448,2560]{1,0:T(8,128)S(1)} fusion(bf16[448,1280]{1,0:T(8,128)(2,1)S(1)} %bitcast.90, bf16[2560,1280]{1,0:T(8,128)(2,1)} %param.8), kind=kOutput, calls=%fused_computation.245 | convolution fusion | flops 2936012800 | bytes 12288000 | tf_op jit(solution)/shard_map/dot_general | solution.py:17
  140.9 5.8 %fusion.71 = f32[256,1280]{1,0:T(8,128)} fusion(bf16[256,2560]{1,0:T(8,128)(2,1)S(1)} %constant_dynamic-update-slice_fusion.14, bf16[1280,2560]{1,0:T(8,128)(2,1)} %param.6), kind=kOutput, calls=%fused_computation.246 | convolution fusion | flops 1677721600 | bytes 9175040 | tf_op jit(solution)/shard_map/dot_general | solution.py:17
  146.8 6.8 %collective-permute-done.17 = bf16[112,2560]{1,0:T(8,128)(2,1)S(1)} collective-permute-done((bf16[112,2560]{1,0:T(8,128)(2,1)S(1)}, bf16[112,2560]{1,0:T(8,128)(2,1)S(1)}, u32[]{:S(2)}, u32[]{:S(2)}) %collective-permute-start.17) | collective-permute-done | bytes 573472 | tf_op jit(solution)/shard_map/ppermute | solution.py:30
  153.6 9.8 %collective-permute-done.18 = bf16[112,2560]{1,0:T(8,128)(2,1)S(1)} collective-permute-done((bf16[112,2560]{1,0:T(8,128)(2,1)S(1)}, bf16[112,2560]{1,0:T(8,128)(2,1)S(1)}, u32[]{:S(2)}, u32[]{:S(2)}) %collective-permute-start.18) | collective-permute-done | bytes 573472 | tf_op jit(solution)/shard_map/ppermute | solution.py:30
  163.4 3.3 collective-permute-done.19
  170.6 4.9 %collective-permute-done.25 = bf16[2,4,1,16,1280]{4,3,1,0,2:T(8,128)(2,1)S(1)} collective-permute-done((bf16[2,4,1,16,1280]{4,3,1,0,2:T(8,128)(2,1)S(1)}, bf16[2,4,1,16,1280]{4,3,1,0,2:T(8,128)(2,1)S(1)}, u32[]{:S(2)}, u32[]{:S(2)}) %collective-permute-start.25) | collective-permute-done | bytes 327712 | tf_op jit(solution)/shard_map/ppermute | solution.py:30
  177.1 8.0 %collective-permute-done.24 = bf16[112,2560]{1,0:T(8,128)(2,1)S(1)} collective-permute-done((bf16[112,2560]{1,0:T(8,128)(2,1)S(1)}, bf16[112,2560]{1,0:T(8,128)(2,1)S(1)}, u32[]{:S(2)}, u32[]{:S(2)}) %collective-permute-start.24) | collective-permute-done | bytes 573472 | tf_op jit(solution)/shard_map/ppermute | solution.py:30
  185.1 10.8 %collective-permute-done.23 = bf16[112,2560]{1,0:T(8,128)(2,1)S(1)} collective-permute-done((bf16[112,2560]{1,0:T(8,128)(2,1)S(1)}, bf16[112,2560]{1,0:T(8,128)(2,1)S(1)}, u32[]{:S(2)}, u32[]{:S(2)}) %collective-permute-start.23) | collective-permute-done | bytes 573472 | tf_op jit(solution)/shard_map/ppermute | solution.py:30
  195.9 2.5 collective-permute-done.20
  202.8 6.6 %fusion.72 = f32[448,2560]{1,0:T(8,128)S(1)} fusion(bf16[448,1280]{1,0:T(8,128)(2,1)S(1)} %bitcast.108, bf16[1280,2560]{1,0:T(8,128)(2,1)} %param.6), kind=kOutput, calls=%fused_computation.247 | convolution fusion | flops 2936012800 | bytes 12288000 | tf_op jit(solution)/shard_map/dot_general | solution.py:91
  215.5 5.7 %fusion.73 = f32[448,2560]{1,0:T(8,128)S(1)} fusion(bf16[448,1280]{1,0:T(8,128)(2,1)S(1)} %bitcast.88, bf16[2560,1280]{1,0:T(8,128)(2,1)} %param.8), kind=kOutput, calls=%fused_computation.248 | convolution fusion | flops 2936012800 | bytes 12288000 | tf_op jit(solution)/shard_map/dot_general | solution.py:17
  223.5 6.0 %collective-permute-done.26 = bf16[112,2560]{1,0:T(8,128)(2,1)S(1)} collective-permute-done((bf16[112,2560]{1,0:T(8,128)(2,1)S(1)}, bf16[112,2560]{1,0:T(8,128)(2,1)S(1)}, u32[]{:S(2)}, u32[]{:S(2)}) %collective-permute-start.26) | collective-permute-done | bytes 573472 | tf_op jit(solution)/shard_map/ppermute | solution.py:30
  229.4 10.1 %collective-permute-done.27 = bf16[112,2560]{1,0:T(8,128)(2,1)S(1)} collective-permute-done((bf16[112,2560]{1,0:T(8,128)(2,1)S(1)}, bf16[112,2560]{1,0:T(8,128)(2,1)S(1)}, u32[]{:S(2)}, u32[]{:S(2)}) %collective-permute-start.27) | collective-permute-done | bytes 573472 | tf_op jit(solution)/shard_map/ppermute | solution.py:30
  239.6 2.9 collective-permute-done.30
  246.5 13.8 %collective-permute-done.35 = bf16[112,2560]{1,0:T(8,128)(2,1)S(1)} collective-permute-done((bf16[112,2560]{1,0:T(8,128)(2,1)S(1)}, bf16[112,2560]{1,0:T(8,128)(2,1)S(1)}, u32[]{:S(2)}, u32[]{:S(2)}) %collective-permute-start.35) | collective-permute-done | bytes 573472 | tf_op jit(solution)/shard_map/ppermute | solution.py:30
  260.4 11.1 %collective-permute-done.34 = bf16[112,2560]{1,0:T(8,128)(2,1)S(1)} collective-permute-done((bf16[112,2560]{1,0:T(8,128)(2,1)S(1)}, bf16[112,2560]{1,0:T(8,128)(2,1)S(1)}, u32[]{:S(2)}, u32[]{:S(2)}) %collective-permute-start.34) | collective-permute-done | bytes 573472 | tf_op jit(solution)/shard_map/ppermute | solution.py:30
  271.5 2.5 collective-permute-done.31
  281.9 3.2 fusion.76
  285.1 5.3 %fusion.74 = f32[448,2560]{1,0:T(8,128)S(1)} fusion(bf16[448,1280]{1,0:T(8,128)(2,1)S(1)} %bitcast.112, bf16[1280,2560]{1,0:T(8,128)(2,1)} %param.6), kind=kOutput, calls=%fused_computation.249 | convolution fusion | flops 2936012800 | bytes 12288000 | tf_op jit(solution)/shard_map/dot_general | solution.py:91
  290.4 7.2 %fusion.75 = f32[448,2560]{1,0:T(8,128)S(1)} fusion(bf16[448,1280]{1,0:T(8,128)(2,1)S(1)} %bitcast.92, bf16[2560,1280]{1,0:T(8,128)(2,1)} %param.8), kind=kOutput, calls=%fused_computation.250 | convolution fusion | flops 2936012800 | bytes 12288000 | tf_op jit(solution)/shard_map/dot_general | solution.py:17
  301.1 2.3 collective-permute-done.37
  308.5 13.8 %collective-permute-done.44 = bf16[112,2560]{1,0:T(8,128)(2,1)S(1)} collective-permute-done((bf16[112,2560]{1,0:T(8,128)(2,1)S(1)}, bf16[112,2560]{1,0:T(8,128)(2,1)S(1)}, u32[]{:S(2)}, u32[]{:S(2)}) %collective-permute-start.44) | collective-permute-done | bytes 573472 | tf_op jit(solution)/shard_map/ppermute | solution.py:30
  322.3 11.3 %collective-permute-done.43 = bf16[112,2560]{1,0:T(8,128)(2,1)S(1)} collective-permute-done((bf16[112,2560]{1,0:T(8,128)(2,1)S(1)}, bf16[112,2560]{1,0:T(8,128)(2,1)S(1)}, u32[]{:S(2)}, u32[]{:S(2)}) %collective-permute-start.43) | collective-permute-done | bytes 573472 | tf_op jit(solution)/shard_map/ppermute | solution.py:30
  340.9 6.2 %fusion.77 = f32[448,1280]{1,0:T(8,128)S(1)} fusion(bf16[448,2560]{1,0:T(8,128)(2,1)S(1)} %get-tuple-element.676, bf16[1280,2560]{1,0:T(8,128)(2,1)} %param.6), kind=kOutput, calls=%fused_computation.252 | convolution fusion | flops 2936012800 | bytes 11141120 | tf_op jit(solution)/shard_map/dot_general | solution.py:17
  347.1 13.1 %fusion.9 = f32[1280,2560]{1,0:T(8,128)} fusion(bf16[1152,2560]{1,0:T(8,128)(2,1)S(1)} %get-tuple-element.675, bf16[448,1280]{1,0:T(8,128)(2,1)S(1)} %bitcast.111, bf16[448,1280]{1,0:T(8,128)(2,1)S(1)} %bitcast.107, bf16[256,1280]{1,0:T(8,128)(2,1)} %bitcast.115), kind=kOutput, calls=%fused_computation.15 | convolution fusion | flops 7558594560 | bytes 21954560 | tf_op jit(solution)/shard_map/dot_general | solution.py:23
  364.8 11.5 %collective-permute-done.47 = bf16[4,2,16,1280]{3,2,0,1:T(8,128)(2,1)S(1)} collective-permute-done((bf16[4,2,16,1280]{3,2,0,1:T(8,128)(2,1)S(1)}, bf16[4,2,16,1280]{3,2,0,1:T(8,128)(2,1)S(1)}, u32[]{:S(2)}, u32[]{:S(2)}) %collective-permute-start.47) | collective-permute-done | bytes 327712 | tf_op jit(solution)/shard_map/ppermute | solution.py:30
  383.6 7.4 %fusion.78 = f32[448,1280]{1,0:T(8,128)} fusion(bf16[448,2560]{1,0:T(8,128)(2,1)S(1)} %constant_dynamic-update-slice_fusion.42, bf16[1280,2560]{1,0:T(8,128)(2,1)} %param.6), kind=kOutput, calls=%fused_computation.253 | convolution fusion | flops 2936012800 | bytes 11141120 | tf_op jit(solution)/shard_map/dot_general | solution.py:17
  392.4 12.0 %fusion = f32[2560,1280]{1,0:T(8,128)} fusion(bf16[1152,1280]{1,0:T(8,128)(2,1)S(1)} %constant_dynamic-update-slice_fusion.44, bf16[448,2560]{1,0:T(8,128)(2,1)S(1)} %pad_maximum_fusion.1, bf16[448,2560]{1,0:T(8,128)(2,1)S(1)} %pad_maximum_fusion, bf16[256,2560]{1,0:T(8,128)(2,1)S(1)} %copy-done.23), kind=kOutput, calls=%fused_computation.4 | convolution fusion | flops 7567441920 | bytes 21954560 | tf_op jit(solution)/shard_map/dot_general | solution.py:23
  407.5 2.7 collective-permute-start.54
  413.8 6.0 %fusion.79 = f32[448,1280]{1,0:T(8,128)S(1)} fusion(bf16[448,2560]{1,0:T(8,128)(2,1)S(1)} %constant_dynamic-update-slice_fusion.47, bf16[1280,2560]{1,0:T(8,128)(2,1)} %param.6), kind=kOutput, calls=%fused_computation.254 | convolution fusion | flops 2936012800 | bytes 11141120 | tf_op jit(solution)/shard_map/dot_general | solution.py:17
  421.1 3.1 collective-permute-done.54
  430.4 12.9 %convolution_add_fusion.1 = f32[1280,2560]{1,0:T(8,128)} fusion(f32[1280,2560]{1,0:T(8,128)} %fusion.9, bf16[896,2560]{1,0:T(8,128)(2,1)S(1)} %constant_dynamic-update-slice_fusion.50, bf16[448,1280]{1,0:T(8,128)(2,1)S(1)} %bitcast.113, bf16[448,1280]{1,0:T(8,128)(2,1)S(1)} %bitcast.109), kind=kOutput, calls=%fused_computation.1 | convolution fusion | flops 5879889920 | bytes 33095680 | tf_op jit(solution)/shard_map/dot_general | solution.py:23
  449.3 13.3 %convolution_add_fusion = f32[2560,1280]{1,0:T(8,128)} fusion(f32[2560,1280]{1,0:T(8,128)} %fusion, bf16[896,1280]{1,0:T(8,128)(2,1)S(1)} %constant_dynamic-update-slice_fusion.52, bf16[448,2560]{1,0:T(8,128)(2,1)S(1)} %pad_maximum_fusion.3, bf16[448,2560]{1,0:T(8,128)(2,1)S(1)} %pad_maximum_fusion.2), kind=kOutput, calls=%fused_computation | convolution fusion | flops 5884477440 | bytes 33095680 | tf_op jit(solution)/shard_map/dot_general | solution.py:23
  464.2 6.7 %collective-permute-done.63 = f32[4,1,16,1280]{3,2,0,1:T(8,128)S(1)} collective-permute-done((f32[4,1,16,1280]{3,2,0,1:T(8,128)S(1)}, f32[4,1,16,1280]{3,2,0,1:T(8,128)S(1)}, u32[]{:S(2)}, u32[]{:S(2)}) %collective-permute-start.63) | collective-permute-done | bytes 327712 | tf_op jit(solution)/shard_map/ppermute | solution.py:30
  (406 shorter events, 119.3 us)
Async XLA Ops:
  21.2 15.9 %collective-permute-start.6 = (bf16[2,4,1,16,1280]{4,3,1,0,2:T(8,128)(2,1)S(1)}, bf16[2,4,1,16,1280]{4,3,1,0,2:T(8,128)(2,1)S(1)}, u32[]{:S(2)}, u32[]{:S(2)}) collective-permute-start(bf16[2,4,1,16,1280]{4,3,1,0,2:T(8,128)(2,1)S(1)} %slice_bitcast_fusion.2), channel_id=1, source_target_pairs={{0,1},{1,0},{2,3},{3,2},{4,5},{5,4},{6,7},{7,6},{8,9},{9,8},{10,11... | collective-permute-start | bytes 983048 | tf_op jit(solution)/shard_map/ppermute | solution.py:30
  23.1 30.6 %collective-permute-start.5 = (bf16[2,4,2,16,1280]{4,3,2,1,0:T(8,128)(2,1)S(1)}, bf16[2,4,2,16,1280]{4,3,2,1,0:T(8,128)(2,1)S(1)}, u32[]{:S(2)}, u32[]{:S(2)}) collective-permute-start(bf16[2,4,2,16,1280]{4,3,2,1,0:T(8,128)(2,1)S(1)} %constant_dynamic-update-slice_fusion), channel_id=1, source_target_pairs={{0,2},{1,3},{2,0},{3,1},{4,6},{5,7},{6,4},{7,5},{8,10},{9,11},{10,... | collective-permute-start | bytes 1966088 | tf_op jit(solution)/shard_map/ppermute | solution.py:30
  53.9 30.8 %collective-permute-start.7 = (bf16[2,4,4,16,1280]{4,3,2,1,0:T(8,128)(2,1)S(1)}, bf16[2,4,4,16,1280]{4,3,2,1,0:T(8,128)(2,1)S(1)}, u32[]{:S(2)}, u32[]{:S(2)}) collective-permute-start(bf16[2,4,4,16,1280]{4,3,2,1,0:T(8,128)(2,1)S(1)} %constant_dynamic-update-slice_fusion.2), channel_id=1, source_target_pairs={{0,16},{16,0},{1,17},{17,1},{2,18},{18,2},{3,19},{19,3},{4,20},{20... | collective-permute-start | bytes 3932168 | tf_op jit(solution)/shard_map/ppermute | solution.py:30
  55.5 29.2 %collective-permute-start.8 = (bf16[2,4,2,16,1280]{4,3,1,0,2:T(8,128)(2,1)S(1)}, bf16[2,4,2,16,1280]{4,3,1,0,2:T(8,128)(2,1)S(1)}, u32[]{:S(2)}, u32[]{:S(2)}) collective-permute-start(bf16[2,4,2,16,1280]{4,3,1,0,2:T(8,128)(2,1)S(1)} %constant_dynamic-update-slice_fusion.4), channel_id=1, source_target_pairs={{0,2},{1,3},{2,0},{3,1},{4,6},{5,7},{6,4},{7,5},{8,10},{9,11},{10,... | collective-permute-start | bytes 1966088 | tf_op jit(solution)/shard_map/ppermute | solution.py:30
  85.1 30.8 %collective-permute-start.11 = (bf16[2,4,4,16,1280]{4,3,1,0,2:T(8,128)(2,1)S(1)}, bf16[2,4,4,16,1280]{4,3,1,0,2:T(8,128)(2,1)S(1)}, u32[]{:S(2)}, u32[]{:S(2)}) collective-permute-start(bf16[2,4,4,16,1280]{4,3,1,0,2:T(8,128)(2,1)S(1)} %constant_dynamic-update-slice_fusion.6), channel_id=1, source_target_pairs={{0,16},{16,0},{1,17},{17,1},{2,18},{18,2},{3,19},{19,3},{4,20},{20... | collective-permute-start | bytes 3932168 | tf_op jit(solution)/shard_map/ppermute | solution.py:30
  135.9 30.8 %collective-permute-start.19 = (bf16[2,4,2,16,1280]{4,3,1,0,2:T(8,128)(2,1)S(1)}, bf16[2,4,2,16,1280]{4,3,1,0,2:T(8,128)(2,1)S(1)}, u32[]{:S(2)}, u32[]{:S(2)}) collective-permute-start(bf16[2,4,2,16,1280]{4,3,1,0,2:T(8,128)(2,1)S(1)} %constant_dynamic-update-slice_fusion.12), channel_id=1, source_target_pairs={{0,2},{1,3},{2,0},{3,1},{4,6},{5,7},{6,4},{7,5},{8,10},{9,11},{10,... | collective-permute-start | bytes 1966088 | tf_op jit(solution)/shard_map/ppermute | solution.py:30
  137.6 16.0 %collective-permute-start.17 = (bf16[112,2560]{1,0:T(8,128)(2,1)S(1)}, bf16[112,2560]{1,0:T(8,128)(2,1)S(1)}, u32[]{:S(2)}, u32[]{:S(2)}) collective-permute-start(bf16[112,2560]{1,0:T(8,128)(2,1)S(1)} %slice.484), channel_id=1, source_target_pairs={{0,8},{4,12},{8,0},{12,4},{1,9},{5,13},{9,1},{13,5},{2,10},{6,14},... | collective-permute-start | bytes 1720328 | tf_op jit(solution)/shard_map/ppermute | solution.py:30
  139.2 24.2 %collective-permute-start.18 = (bf16[112,2560]{1,0:T(8,128)(2,1)S(1)}, bf16[112,2560]{1,0:T(8,128)(2,1)S(1)}, u32[]{:S(2)}, u32[]{:S(2)}) collective-permute-start(bf16[112,2560]{1,0:T(8,128)(2,1)S(1)} %slice.483), channel_id=1, source_target_pairs={{0,8},{4,12},{8,0},{12,4},{1,9},{5,13},{9,1},{13,5},{2,10},{6,14},... | collective-permute-start | bytes 1720328 | tf_op jit(solution)/shard_map/ppermute | solution.py:30
  166.9 29.0 %collective-permute-start.21 = (bf16[224,2560]{1,0:T(8,128)(2,1)S(1)}, bf16[224,2560]{1,0:T(8,128)(2,1)S(1)}, u32[]{:S(2)}, u32[]{:S(2)}) collective-permute-start(bf16[224,2560]{1,0:T(8,128)(2,1)S(1)} %slice.472), channel_id=1, source_target_pairs={{0,4},{4,0},{8,12},{12,8},{1,5},{5,1},{9,13},{13,9},{2,6},{6,2},{1... | collective-permute-start | bytes 3440648 | tf_op jit(solution)/shard_map/ppermute | solution.py:30
  166.9 28.9 %collective-permute-start.22 = (bf16[224,2560]{1,0:T(8,128)(2,1)S(1)}, bf16[224,2560]{1,0:T(8,128)(2,1)S(1)}, u32[]{:S(2)}, u32[]{:S(2)}) collective-permute-start(bf16[224,2560]{1,0:T(8,128)(2,1)S(1)} %slice.471), channel_id=1, source_target_pairs={{0,4},{4,0},{8,12},{12,8},{1,5},{5,1},{9,13},{13,9},{2,6},{6,2},{1... | collective-permute-start | bytes 3440648 | tf_op jit(solution)/shard_map/ppermute | solution.py:30
  167.5 30.8 %collective-permute-start.20 = (bf16[2,4,4,16,1280]{4,3,1,0,2:T(8,128)(2,1)S(1)}, bf16[2,4,4,16,1280]{4,3,1,0,2:T(8,128)(2,1)S(1)}, u32[]{:S(2)}, u32[]{:S(2)}) collective-permute-start(bf16[2,4,4,16,1280]{4,3,1,0,2:T(8,128)(2,1)S(1)} %constant_dynamic-update-slice_fusion.16), channel_id=1, source_target_pairs={{0,16},{16,0},{1,17},{17,1},{2,18},{18,2},{3,19},{19,3},{4,20},{20... | collective-permute-start | bytes 3932168 | tf_op jit(solution)/shard_map/ppermute | solution.py:30
  169.1 16.0 %collective-permute-start.24 = (bf16[112,2560]{1,0:T(8,128)(2,1)S(1)}, bf16[112,2560]{1,0:T(8,128)(2,1)S(1)}, u32[]{:S(2)}, u32[]{:S(2)}) collective-permute-start(bf16[112,2560]{1,0:T(8,128)(2,1)S(1)} %get-tuple-element.427), channel_id=1, source_target_pairs={{0,8},{4,12},{8,0},{12,4},{1,9},{5,13},{9,1},{13,5},{2,10},{6,14},... | collective-permute-start | bytes 1720328 | tf_op jit(solution)/shard_map/ppermute | solution.py:30
  175.6 20.3 %collective-permute-start.23 = (bf16[112,2560]{1,0:T(8,128)(2,1)S(1)}, bf16[112,2560]{1,0:T(8,128)(2,1)S(1)}, u32[]{:S(2)}, u32[]{:S(2)}) collective-permute-start(bf16[112,2560]{1,0:T(8,128)(2,1)S(1)} %get-tuple-element.425), channel_id=1, source_target_pairs={{0,8},{4,12},{8,0},{12,4},{1,9},{5,13},{9,1},{13,5},{2,10},{6,14},... | collective-permute-start | bytes 1720328 | tf_op jit(solution)/shard_map/ppermute | solution.py:30
  198.9 43.5 %collective-permute-start.29 = (bf16[224,2560]{1,0:T(8,128)(2,1)S(1)}, bf16[224,2560]{1,0:T(8,128)(2,1)S(1)}, u32[]{:S(2)}, u32[]{:S(2)}) collective-permute-start(bf16[224,2560]{1,0:T(8,128)(2,1)S(1)} %constant_dynamic-update-slice_fusion.20), channel_id=1, source_target_pairs={{0,4},{4,0},{8,12},{12,8},{1,5},{5,1},{9,13},{13,9},{2,6},{6,2},{1... | collective-permute-start | bytes 3440648 | tf_op jit(solution)/shard_map/ppermute | solution.py:30
  199.0 43.4 %collective-permute-start.28 = (bf16[224,2560]{1,0:T(8,128)(2,1)S(1)}, bf16[224,2560]{1,0:T(8,128)(2,1)S(1)}, u32[]{:S(2)}, u32[]{:S(2)}) collective-permute-start(bf16[224,2560]{1,0:T(8,128)(2,1)S(1)} %constant_dynamic-update-slice_fusion.18), channel_id=1, source_target_pairs={{0,4},{4,0},{8,12},{12,8},{1,5},{5,1},{9,13},{13,9},{2,6},{6,2},{1... | collective-permute-start | bytes 3440648 | tf_op jit(solution)/shard_map/ppermute | solution.py:30
  211.6 30.9 %collective-permute-start.30 = (bf16[2,4,2,16,1280]{4,3,1,0,2:T(8,128)(2,1)S(1)}, bf16[2,4,2,16,1280]{4,3,1,0,2:T(8,128)(2,1)S(1)}, u32[]{:S(2)}, u32[]{:S(2)}) collective-permute-start(bf16[2,4,2,16,1280]{4,3,1,0,2:T(8,128)(2,1)S(1)} %constant_dynamic-update-slice_fusion.22), channel_id=1, source_target_pairs={{0,2},{1,3},{2,0},{3,1},{4,6},{5,7},{6,4},{7,5},{8,10},{9,11},{10,... | collective-permute-start | bytes 1966088 | tf_op jit(solution)/shard_map/ppermute | solution.py:30
  213.5 16.0 %collective-permute-start.26 = (bf16[112,2560]{1,0:T(8,128)(2,1)S(1)}, bf16[112,2560]{1,0:T(8,128)(2,1)S(1)}, u32[]{:S(2)}, u32[]{:S(2)}) collective-permute-start(bf16[112,2560]{1,0:T(8,128)(2,1)S(1)} %slice.482), channel_id=1, source_target_pairs={{0,8},{4,12},{8,0},{12,4},{1,9},{5,13},{9,1},{13,5},{2,10},{6,14},... | collective-permute-start | bytes 1720328 | tf_op jit(solution)/shard_map/ppermute | solution.py:30
  215.0 24.5 %collective-permute-start.27 = (bf16[112,2560]{1,0:T(8,128)(2,1)S(1)}, bf16[112,2560]{1,0:T(8,128)(2,1)S(1)}, u32[]{:S(2)}, u32[]{:S(2)}) collective-permute-start(bf16[112,2560]{1,0:T(8,128)(2,1)S(1)} %slice.481), channel_id=1, source_target_pairs={{0,8},{4,12},{8,0},{12,4},{1,9},{5,13},{9,1},{13,5},{2,10},{6,14},... | collective-permute-start | bytes 1720328 | tf_op jit(solution)/shard_map/ppermute | solution.py:30
  242.4 29.0 %collective-permute-start.32 = (bf16[224,2560]{1,0:T(8,128)(2,1)S(1)}, bf16[224,2560]{1,0:T(8,128)(2,1)S(1)}, u32[]{:S(2)}, u32[]{:S(2)}) collective-permute-start(bf16[224,2560]{1,0:T(8,128)(2,1)S(1)} %slice.470), channel_id=1, source_target_pairs={{0,4},{4,0},{8,12},{12,8},{1,5},{5,1},{9,13},{13,9},{2,6},{6,2},{1... | collective-permute-start | bytes 3440648 | tf_op jit(solution)/shard_map/ppermute | solution.py:30
  242.5 29.0 %collective-permute-start.33 = (bf16[224,2560]{1,0:T(8,128)(2,1)S(1)}, bf16[224,2560]{1,0:T(8,128)(2,1)S(1)}, u32[]{:S(2)}, u32[]{:S(2)}) collective-permute-start(bf16[224,2560]{1,0:T(8,128)(2,1)S(1)} %slice.469), channel_id=1, source_target_pairs={{0,4},{4,0},{8,12},{12,8},{1,5},{5,1},{9,13},{13,9},{2,6},{6,2},{1... | collective-permute-start | bytes 3440648 | tf_op jit(solution)/shard_map/ppermute | solution.py:30
  243.1 30.8 %collective-permute-start.31 = (bf16[2,4,4,16,1280]{4,3,1,0,2:T(8,128)(2,1)S(1)}, bf16[2,4,4,16,1280]{4,3,1,0,2:T(8,128)(2,1)S(1)}, u32[]{:S(2)}, u32[]{:S(2)}) collective-permute-start(bf16[2,4,4,16,1280]{4,3,1,0,2:T(8,128)(2,1)S(1)} %constant_dynamic-update-slice_fusion.24), channel_id=1, source_target_pairs={{0,16},{16,0},{1,17},{17,1},{2,18},{18,2},{3,19},{19,3},{4,20},{20... | collective-permute-start | bytes 3932168 | tf_op jit(solution)/shard_map/ppermute | solution.py:30
  244.5 15.9 %collective-permute-start.35 = (bf16[112,2560]{1,0:T(8,128)(2,1)S(1)}, bf16[112,2560]{1,0:T(8,128)(2,1)S(1)}, u32[]{:S(2)}, u32[]{:S(2)}) collective-permute-start(bf16[112,2560]{1,0:T(8,128)(2,1)S(1)} %get-tuple-element.479), channel_id=1, source_target_pairs={{0,8},{4,12},{8,0},{12,4},{1,9},{5,13},{9,1},{13,5},{2,10},{6,14},... | collective-permute-start | bytes 1720328 | tf_op jit(solution)/shard_map/ppermute | solution.py:30
  246.0 25.5 %collective-permute-start.34 = (bf16[112,2560]{1,0:T(8,128)(2,1)S(1)}, bf16[112,2560]{1,0:T(8,128)(2,1)S(1)}, u32[]{:S(2)}, u32[]{:S(2)}) collective-permute-start(bf16[112,2560]{1,0:T(8,128)(2,1)S(1)} %get-tuple-element.477), channel_id=1, source_target_pairs={{0,8},{4,12},{8,0},{12,4},{1,9},{5,13},{9,1},{13,5},{2,10},{6,14},... | collective-permute-start | bytes 1720328 | tf_op jit(solution)/shard_map/ppermute | solution.py:30
  274.6 28.9 %collective-permute-start.39 = (bf16[224,2560]{1,0:T(8,128)(2,1)S(1)}, bf16[224,2560]{1,0:T(8,128)(2,1)}, u32[]{:S(2)}, u32[]{:S(2)}) collective-permute-start(bf16[224,2560]{1,0:T(8,128)(2,1)S(1)} %constant_dynamic-update-slice_fusion.28), channel_id=1, source_target_pairs={{0,4},{4,0},{8,12},{12,8},{1,5},{5,1},{9,13},{13,9},{2,6},{6,2},{1... | collective-permute-start | bytes 3440648 | tf_op jit(solution)/shard_map/ppermute | solution.py:30
  274.7 28.8 %collective-permute-start.38 = (bf16[224,2560]{1,0:T(8,128)(2,1)S(1)}, bf16[224,2560]{1,0:T(8,128)(2,1)}, u32[]{:S(2)}, u32[]{:S(2)}) collective-permute-start(bf16[224,2560]{1,0:T(8,128)(2,1)S(1)} %constant_dynamic-update-slice_fusion.26), channel_id=1, source_target_pairs={{0,4},{4,0},{8,12},{12,8},{1,5},{5,1},{9,13},{13,9},{2,6},{6,2},{1... | collective-permute-start | bytes 3440648 | tf_op jit(solution)/shard_map/ppermute | solution.py:30
  276.9 24.3 %collective-permute-start.36 = (bf16[112,2560]{1,0:T(8,128)(2,1)S(1)}, bf16[112,2560]{1,0:T(8,128)(2,1)}, u32[]{:S(2)}, u32[]{:S(2)}) collective-permute-start(bf16[112,2560]{1,0:T(8,128)(2,1)S(1)} %slice.480), channel_id=1, source_target_pairs={{0,8},{4,12},{8,0},{12,4},{1,9},{5,13},{9,1},{13,5},{2,10},{6,14},... | collective-permute-start | bytes 1720328 | tf_op jit(solution)/shard_map/ppermute | solution.py:30
  280.1 23.3 %collective-permute-start.37 = (bf16[112,2560]{1,0:T(8,128)(2,1)}, bf16[112,2560]{1,0:T(8,128)(2,1)}, u32[]{:S(2)}, u32[]{:S(2)}) collective-permute-start(bf16[112,2560]{1,0:T(8,128)(2,1)} %slice.479), channel_id=1, source_target_pairs={{0,8},{4,12},{8,0},{12,4},{1,9},{5,13},{9,1},{13,5},{2,10},{6,14},... | collective-permute-start | bytes 1720328 | tf_op jit(solution)/shard_map/ppermute | solution.py:30
  303.4 30.2 %collective-permute-start.42 = (bf16[4,4,16,1280]{3,2,0,1:T(8,128)(2,1)S(1)}, bf16[4,4,16,1280]{3,2,0,1:T(8,128)(2,1)S(1)}, u32[]{:S(2)}, u32[]{:S(2)}) collective-permute-start(bf16[4,4,16,1280]{3,2,0,1:T(8,128)(2,1)S(1)} %copy.47), channel_id=1, source_target_pairs={{0,16},{16,0},{1,17},{17,1},{2,18},{18,2},{3,19},{19,3},{4,20},{20... | collective-permute-start | bytes 1966088 | tf_op jit(solution)/shard_map/ppermute | solution.py:30
  304.0 29.7 %collective-permute-start.40 = (bf16[224,2560]{1,0:T(8,128)(2,1)S(1)}, bf16[224,2560]{1,0:T(8,128)(2,1)S(1)}, u32[]{:S(2)}, u32[]{:S(2)}) collective-permute-start(bf16[224,2560]{1,0:T(8,128)(2,1)S(1)} %slice.468), channel_id=1, source_target_pairs={{0,4},{4,0},{8,12},{12,8},{1,5},{5,1},{9,13},{13,9},{2,6},{6,2},{1... | collective-permute-start | bytes 3440648 | tf_op jit(solution)/shard_map/ppermute | solution.py:30
  304.0 29.7 %collective-permute-start.41 = (bf16[224,2560]{1,0:T(8,128)(2,1)S(1)}, bf16[224,2560]{1,0:T(8,128)(2,1)S(1)}, u32[]{:S(2)}, u32[]{:S(2)}) collective-permute-start(bf16[224,2560]{1,0:T(8,128)(2,1)S(1)} %slice.467), channel_id=1, source_target_pairs={{0,4},{4,0},{8,12},{12,8},{1,5},{5,1},{9,13},{13,9},{2,6},{6,2},{1... | collective-permute-start | bytes 3440648 | tf_op jit(solution)/shard_map/ppermute | solution.py:30
  306.4 15.9 %collective-permute-start.44 = (bf16[112,2560]{1,0:T(8,128)(2,1)S(1)}, bf16[112,2560]{1,0:T(8,128)(2,1)S(1)}, u32[]{:S(2)}, u32[]{:S(2)}) collective-permute-start(bf16[112,2560]{1,0:T(8,128)(2,1)S(1)} %get-tuple-element.541), channel_id=1, source_target_pairs={{0,8},{4,12},{8,0},{12,4},{1,9},{5,13},{9,1},{13,5},{2,10},{6,14},... | collective-permute-start | bytes 1720328 | tf_op jit(solution)/shard_map/ppermute | solution.py:30
  308.0 25.7 %collective-permute-start.43 = (bf16[112,2560]{1,0:T(8,128)(2,1)S(1)}, bf16[112,2560]{1,0:T(8,128)(2,1)S(1)}, u32[]{:S(2)}, u32[]{:S(2)}) collective-permute-start(bf16[112,2560]{1,0:T(8,128)(2,1)S(1)} %get-tuple-element.539), channel_id=1, source_target_pairs={{0,8},{4,12},{8,0},{12,4},{1,9},{5,13},{9,1},{13,5},{2,10},{6,14},... | collective-permute-start | bytes 1720328 | tf_op jit(solution)/shard_map/ppermute | solution.py:30
  334.0 42.3 %collective-permute-start.49 = (bf16[224,2560]{1,0:T(8,128)(2,1)S(1)}, bf16[224,2560]{1,0:T(8,128)(2,1)}, u32[]{:S(2)}, u32[]{:S(2)}) collective-permute-start(bf16[224,2560]{1,0:T(8,128)(2,1)S(1)} %constant_dynamic-update-slice_fusion.34), channel_id=1, source_target_pairs={{0,4},{4,0},{8,12},{12,8},{1,5},{5,1},{9,13},{13,9},{2,6},{6,2},{1... | collective-permute-start | bytes 3440648 | tf_op jit(solution)/shard_map/ppermute | solution.py:30
  334.1 42.2 %collective-permute-start.48 = (bf16[224,2560]{1,0:T(8,128)(2,1)S(1)}, bf16[224,2560]{1,0:T(8,128)(2,1)}, u32[]{:S(2)}, u32[]{:S(2)}) collective-permute-start(bf16[224,2560]{1,0:T(8,128)(2,1)S(1)} %constant_dynamic-update-slice_fusion.32), channel_id=1, source_target_pairs={{0,4},{4,0},{8,12},{12,8},{1,5},{5,1},{9,13},{13,9},{2,6},{6,2},{1... | collective-permute-start | bytes 3440648 | tf_op jit(solution)/shard_map/ppermute | solution.py:30
  336.8 39.5 %collective-permute-start.45 = (bf16[112,2560]{1,0:T(8,128)(2,1)}, bf16[112,2560]{1,0:T(8,128)(2,1)}, u32[]{:S(2)}, u32[]{:S(2)}) collective-permute-start(bf16[112,2560]{1,0:T(8,128)(2,1)} %slice.478), channel_id=1, source_target_pairs={{0,8},{4,12},{8,0},{12,4},{1,9},{5,13},{9,1},{13,5},{2,10},{6,14},... | collective-permute-start | bytes 1720328 | tf_op jit(solution)/shard_map/ppermute | solution.py:30
  360.7 15.6 %collective-permute-start.47 = (bf16[4,2,16,1280]{3,2,0,1:T(8,128)(2,1)S(1)}, bf16[4,2,16,1280]{3,2,0,1:T(8,128)(2,1)S(1)}, u32[]{:S(2)}, u32[]{:S(2)}) collective-permute-start(bf16[4,2,16,1280]{3,2,0,1:T(8,128)(2,1)S(1)} %slice.488), channel_id=1, source_target_pairs={{0,2},{1,3},{2,0},{3,1},{4,6},{5,7},{6,4},{7,5},{8,10},{9,11},{10,... | collective-permute-start | bytes 983048 | tf_op jit(solution)/shard_map/ppermute | solution.py:30
  360.8 15.5 %collective-permute-start.46 = (bf16[112,2560]{1,0:T(8,128)(2,1)S(1)}, bf16[112,2560]{1,0:T(8,128)(2,1)S(1)}, u32[]{:S(2)}, u32[]{:S(2)}) collective-permute-start(bf16[112,2560]{1,0:T(8,128)(2,1)S(1)} %slice.477), channel_id=1, source_target_pairs={{0,8},{4,12},{8,0},{12,4},{1,9},{5,13},{9,1},{13,5},{2,10},{6,14},... | collective-permute-start | bytes 1720328 | tf_op jit(solution)/shard_map/ppermute | solution.py:30
  376.4 30.8 %collective-permute-start.50 = (f32[4,1,16,1280]{3,2,0,1:T(8,128)S(1)}, f32[4,1,16,1280]{3,2,0,1:T(8,128)S(1)}, u32[]{:S(2)}, u32[]{:S(2)}) collective-permute-start(f32[4,1,16,1280]{3,2,0,1:T(8,128)S(1)} %get-tuple-element.691), channel_id=1, source_target_pairs={{0,1},{1,0},{2,3},{3,2},{4,5},{5,4},{6,7},{7,6},{8,9},{9,8},{10,11... | collective-permute-start | bytes 983048 | tf_op jit(solution)/shard_map/ppermute | solution.py:30
  376.7 30.5 %collective-permute-start.51 = (bf16[4,4,16,1280]{3,2,0,1:T(8,128)(2,1)S(1)}, bf16[4,4,16,1280]{3,2,0,1:T(8,128)(2,1)S(1)}, u32[]{:S(2)}, u32[]{:S(2)}) collective-permute-start(bf16[4,4,16,1280]{3,2,0,1:T(8,128)(2,1)S(1)} %copy.46), channel_id=1, source_target_pairs={{0,16},{16,0},{1,17},{17,1},{2,18},{18,2},{3,19},{19,3},{4,20},{20... | collective-permute-start | bytes 1966088 | tf_op jit(solution)/shard_map/ppermute | solution.py:30
  380.1 27.1 %collective-permute-start.53 = (bf16[112,2560]{1,0:T(8,128)(2,1)S(1)}, bf16[112,2560]{1,0:T(8,128)(2,1)S(1)}, u32[]{:S(2)}, u32[]{:S(2)}) collective-permute-start(bf16[112,2560]{1,0:T(8,128)(2,1)S(1)} %get-tuple-element.593), channel_id=1, source_target_pairs={{0,8},{4,12},{8,0},{12,4},{1,9},{5,13},{9,1},{13,5},{2,10},{6,14},... | collective-permute-start | bytes 1720328 | tf_op jit(solution)/shard_map/ppermute | solution.py:30
  381.6 25.6 %collective-permute-start.52 = (bf16[112,2560]{1,0:T(8,128)(2,1)S(1)}, bf16[112,2560]{1,0:T(8,128)(2,1)S(1)}, u32[]{:S(2)}, u32[]{:S(2)}) collective-permute-start(bf16[112,2560]{1,0:T(8,128)(2,1)S(1)} %get-tuple-element.591), channel_id=1, source_target_pairs={{0,8},{4,12},{8,0},{12,4},{1,9},{5,13},{9,1},{13,5},{2,10},{6,14},... | collective-permute-start | bytes 1720328 | tf_op jit(solution)/shard_map/ppermute | solution.py:30
  407.5 16.6 %collective-permute-start.54 = (bf16[4,2,16,1280]{3,2,0,1:T(8,128)(2,1)S(1)}, bf16[4,2,16,1280]{3,2,0,1:T(8,128)(2,1)S(1)}, u32[]{:S(2)}, u32[]{:S(2)}) collective-permute-start(bf16[4,2,16,1280]{3,2,0,1:T(8,128)(2,1)S(1)} %slice.487), channel_id=1, source_target_pairs={{0,2},{1,3},{2,0},{3,1},{4,6},{5,7},{6,4},{7,5},{8,10},{9,11},{10,... | collective-permute-start | bytes 983048 | tf_op jit(solution)/shard_map/ppermute | solution.py:30
  410.3 15.3 %collective-permute-start.55 = (bf16[4,4,16,1280]{3,2,0,1:T(8,128)(2,1)S(1)}, bf16[4,4,16,1280]{3,2,0,1:T(8,128)(2,1)S(1)}, u32[]{:S(2)}, u32[]{:S(2)}) collective-permute-start(bf16[4,4,16,1280]{3,2,0,1:T(8,128)(2,1)S(1)} %copy.45), channel_id=1, source_target_pairs={{0,16},{16,0},{1,17},{17,1},{2,18},{18,2},{3,19},{19,3},{4,20},{20... | collective-permute-start | bytes 1966088 | tf_op jit(solution)/shard_map/ppermute | solution.py:30
  425.8 18.8 %collective-permute-start.59 = (bf16[4,2,16,1280]{3,2,0,1:T(8,128)(2,1)S(1)}, bf16[4,2,16,1280]{3,2,0,1:T(8,128)(2,1)}, u32[]{:S(2)}, u32[]{:S(2)}) collective-permute-start(bf16[4,2,16,1280]{3,2,0,1:T(8,128)(2,1)S(1)} %slice.486), channel_id=1, source_target_pairs={{0,2},{1,3},{2,0},{3,1},{4,6},{5,7},{6,4},{7,5},{8,10},{9,11},{10,... | collective-permute-start | bytes 983048 | tf_op jit(solution)/shard_map/ppermute | solution.py:30
  426.4 18.3 %collective-permute-start.58 = (f32[4,1,16,1280]{3,2,0,1:T(8,128)S(1)}, f32[4,1,16,1280]{3,2,0,1:T(8,128)}, u32[]{:S(2)}, u32[]{:S(2)}) collective-permute-start(f32[4,1,16,1280]{3,2,0,1:T(8,128)S(1)} %get-tuple-element.689), channel_id=1, source_target_pairs={{0,1},{1,0},{2,3},{3,2},{4,5},{5,4},{6,7},{7,6},{8,9},{9,8},{10,11... | collective-permute-start | bytes 983048 | tf_op jit(solution)/shard_map/ppermute | solution.py:30
  428.1 16.6 %collective-permute-start.60 = (bf16[4,4,16,1280]{3,2,0,1:T(8,128)(2,1)}, bf16[4,4,16,1280]{3,2,0,1:T(8,128)(2,1)S(1)}, u32[]{:S(2)}, u32[]{:S(2)}) collective-permute-start(bf16[4,4,16,1280]{3,2,0,1:T(8,128)(2,1)} %copy.44), channel_id=1, source_target_pairs={{0,16},{16,0},{1,17},{17,1},{2,18},{18,2},{3,19},{19,3},{4,20},{20... | collective-permute-start | bytes 1966088 | tf_op jit(solution)/shard_map/ppermute | solution.py:30
  445.0 18.6 %collective-permute-start.62 = (bf16[4,2,16,1280]{3,2,0,1:T(8,128)(2,1)S(1)}, bf16[4,2,16,1280]{3,2,0,1:T(8,128)(2,1)S(1)}, u32[]{:S(2)}, u32[]{:S(2)}) collective-permute-start(bf16[4,2,16,1280]{3,2,0,1:T(8,128)(2,1)S(1)} %slice.485), channel_id=1, source_target_pairs={{0,2},{1,3},{2,0},{3,1},{4,6},{5,7},{6,4},{7,5},{8,10},{9,11},{10,... | collective-permute-start | bytes 983048 | tf_op jit(solution)/shard_map/ppermute | solution.py:30
  447.4 16.2 %collective-permute-start.61 = (f32[4,1,16,1280]{3,2,0,1:T(8,128)S(1)}, f32[4,1,16,1280]{3,2,0,1:T(8,128)S(1)}, u32[]{:S(2)}, u32[]{:S(2)}) collective-permute-start(f32[4,1,16,1280]{3,2,0,1:T(8,128)S(1)} %get-tuple-element.687), channel_id=1, source_target_pairs={{0,1},{1,0},{2,3},{3,2},{4,5},{5,4},{6,7},{7,6},{8,9},{9,8},{10,11... | collective-permute-start | bytes 983048 | tf_op jit(solution)/shard_map/ppermute | solution.py:30
  (81 other events, 535.1 us)
